TPU v7x, 32 devices: a whole 2x2x4 slice. The times are simulated.
32 devices in a mesh: exp: 8 (over y, x, core), seq: 4 (over z).
Axes of the slice: x: 2, y: 2, z: 4, core: 2. Of those that a mesh axis runs over, the one named last changes fastest.
Arguments:
- tokens: bfloat16 [16, 1024, 768], P('exp', 'seq'), may hold values from -6 to 6
- cotangent: bfloat16 [16, 1024, 768], P('exp', 'seq'), may hold values from -6 to 6
- token_ids: int32 [16, 1024], P('exp', 'seq'), may hold values from 0 to 50256, as said below
- segments: int32 [16, 1024], P('exp'), may hold values from 0 to 4, as said below
- hash_table: int32 [50257], replicated, may hold values from 0 to 7
- w_qkv: bfloat16 [768, 2304], P(('exp', 'seq')), may hold values from -0.21875 to 0.21875
- w_attn_out: bfloat16 [768, 768], P(('exp', 'seq')), may hold values from -1.75 to 1.75
- norm_scale: bfloat16 [768, 2], P(('exp', 'seq')), may hold values from 0.099609375 to 1.8984375
- norm_shift: bfloat16 [768, 2], P(('exp', 'seq')), may hold values from -3 to 3
- w_in: bfloat16 [8, 768, 3072], P('exp'), may hold values from -0.21875 to 0.21875
- w_out: bfloat16 [8, 3072, 768], P('exp'), may hold values from -0.109375 to 0.109375
Outputs:
- layer_out: bfloat16 [16, 1024, 768], P('exp', 'seq')
- grad_tokens: float32 [16, 1024, 768], P('exp', 'seq')
- grad_w_qkv: float32 [768, 2304], P(('exp', 'seq'))
- grad_w_attn_out: float32 [768, 768], P(('exp', 'seq'))
- grad_norm_scale: float32 [768, 2], P(('exp', 'seq'))
- grad_norm_shift: float32 [768, 2], P(('exp', 'seq'))
- grad_w_in: float32 [8, 768, 3072], P('exp', None, 'seq')
- grad_w_out: float32 [8, 3072, 768], P('exp', 'seq')
Inputs may be any that keep to these rules, and one draw needn't show every extreme that they name: `token_ids`: the rows of one device name at most 192 tokens that the table sends to one expert, and one expert gets exactly 192 from every device. `segments`: never falling along a sequence; in each sequence one document begins within the first 256 positions and ends within the last 256.
All inputs are finite; a program needn't handle non-finite values.
Results may differ from a plain program's by a relative error of at most 0.012.
Values may be sent and summed in bfloat16 or wider, within the bound.
No kernel may reach another device: no remote copies, remote signals or barrier semaphores. Data moves between devices by JAX's collectives and lax.ppermute only.
A program may use at most 256 MiB of HBM per device.

v0:
```python
import jax
import jax.numpy as jnp
from jax import lax
from jax.sharding import PartitionSpec as P

HEAD_DIM = 64


epsilon = 1e-05


def layer_norm(feature, gain_col, bias_col):
    center = feature - jnp.mean(feature, axis=-1, keepdims=True)
    spread = jnp.mean(center * center, axis=-1, keepdims=True)
    return center * lax.rsqrt(spread + epsilon) * gain_col + bias_col


def gelu_tanh(feature):
    return jax.nn.gelu(feature, approximate=True)


def local(
    tokens,
    cotangent,
    token_ids,
    segments,
    hash_table,
    w_qkv,
    w_attn_out,
    norm_scale,
    norm_shift,
    w_in,
    w_out,
):
    seq_dev, rows_seq, model_width = tokens.shape
    row_count = seq_dev * rows_seq
    seq_parts = lax.axis_size("seq")
    owners = lax.axis_size("exp")
    slot_rows = 3 * row_count // owners
    full_len = rows_seq * seq_parts
    head_dim = HEAD_DIM
    head_count = model_width // head_dim
    score_scale = head_dim ** (-0.5)
    full_qkv, full_out, full_gain, full_bias = (
        lax.all_gather(w_qkv, ("exp", "seq"), axis=0, tiled=True),
        lax.all_gather(w_attn_out, ("exp", "seq"), axis=0, tiled=True),
        lax.all_gather(norm_scale, ("exp", "seq"), axis=0, tiled=True),
        lax.all_gather(norm_shift, ("exp", "seq"), axis=0, tiled=True),
    )
    norm_gain = full_gain.astype(jnp.float32)
    norm_bias = full_bias.astype(jnp.float32)
    tok_rows = tokens.reshape(row_count, model_width).astype(jnp.float32)
    normed_low = layer_norm(tok_rows, norm_gain[:, 0], norm_bias[:, 0]).astype(jnp.bfloat16)
    qkv_low = jnp.dot(normed_low, full_qkv, preferred_element_type=jnp.float32).astype(jnp.bfloat16)
    queries = qkv_low[:, :model_width].reshape(seq_dev, rows_seq, head_count, head_dim)
    key_local = qkv_low[:, model_width : 2 * model_width].reshape(seq_dev, rows_seq, model_width)
    value_local = qkv_low[:, 2 * model_width :].reshape(seq_dev, rows_seq, model_width)
    key_full, value_full = (
        lax.all_gather(key_local, "seq", axis=1, tiled=True),
        lax.all_gather(value_local, "seq", axis=1, tiled=True),
    )
    row_start = lax.axis_index("seq") * rows_seq
    q_position = row_start + jnp.arange(rows_seq, dtype=jnp.int32)
    k_position = jnp.arange(full_len, dtype=jnp.int32)
    seg_query = lax.dynamic_slice_in_dim(segments, row_start, rows_seq, 1)
    allowed = (k_position[None, None, :] <= q_position[None, :, None]) & (
        seg_query[:, :, None] == segments[:, None, :]
    )

    def scores_of(key_block):
        shaped_keys = key_block.reshape(seq_dev, full_len, head_count, head_dim)
        scores = (
            jnp.einsum("sqhd,skhd->shqk", queries, shaped_keys, preferred_element_type=jnp.float32)
            * score_scale
        )
        return jnp.where(allowed[:, None], scores, -1e30)

    scores = scores_of(key_full)
    row_max = jnp.max(scores, axis=-1, keepdims=True)
    expo = jnp.exp(scores - row_max)
    row_sum = jnp.sum(expo, axis=-1, keepdims=True)
    probs_fwd = expo / row_sum
    log_total = row_max + jnp.log(row_sum)
    value_heads = value_full.reshape(seq_dev, full_len, head_count, head_dim)
    attended = jnp.einsum(
        "shqk,skhd->sqhd",
        probs_fwd.astype(jnp.bfloat16),
        value_heads,
        preferred_element_type=jnp.float32,
    )
    att_low = attended.reshape(row_count, model_width).astype(jnp.bfloat16)
    middle = tok_rows + jnp.dot(att_low, full_out, preferred_element_type=jnp.float32)
    sent = layer_norm(middle, norm_gain[:, 1], norm_bias[:, 1]).astype(jnp.bfloat16)
    expert = hash_table[token_ids.reshape(-1)]
    onehot = (expert[:, None] == jnp.arange(owners, dtype=jnp.int32)[None, :]).astype(jnp.int32)
    slot_rank = jnp.sum(jnp.cumsum(onehot, axis=0) * onehot, axis=1) - 1
    slot_index = expert * slot_rows + slot_rank
    packed = jnp.zeros((owners * slot_rows, model_width), jnp.bfloat16).at[slot_index].set(sent)
    arrived = lax.all_to_all(
        packed.reshape(owners, slot_rows, model_width),
        "exp",
        split_axis=0,
        concat_axis=0,
        tiled=True,
    )
    arrived = arrived.reshape(owners * slot_rows, model_width)
    hidden_pre = jnp.dot(arrived, w_in[0], preferred_element_type=jnp.float32)
    hidden_act = gelu_tanh(hidden_pre).astype(jnp.bfloat16)
    expert_out = jnp.dot(hidden_act, w_out[0], preferred_element_type=jnp.float32).astype(
        jnp.bfloat16
    )
    returned = lax.all_to_all(
        expert_out.reshape(owners, slot_rows, model_width),
        "exp",
        split_axis=0,
        concat_axis=0,
        tiled=True,
    )
    expert_rows = returned.reshape(owners * slot_rows, model_width)[slot_index].astype(jnp.float32)
    layer_out = (middle + expert_rows).astype(jnp.bfloat16).reshape(seq_dev, rows_seq, model_width)
    grad_low = cotangent.reshape(row_count, model_width)
    grad_out = grad_low.astype(jnp.float32)
    grad_packed = (
        jnp.zeros((owners * slot_rows, model_width), jnp.bfloat16).at[slot_index].set(grad_low)
    )
    grad_arrived = lax.all_to_all(
        grad_packed.reshape(owners, slot_rows, model_width),
        "exp",
        split_axis=0,
        concat_axis=0,
        tiled=True,
    )
    grad_arrived = grad_arrived.reshape(owners * slot_rows, model_width)
    gelu_pull = jax.vjp(gelu_tanh, hidden_pre)[1]
    grad_act = jnp.dot(grad_arrived, w_out[0].T, preferred_element_type=jnp.float32)
    grad_pre = gelu_pull(grad_act)[0].astype(jnp.bfloat16)
    grad_inner = jnp.einsum("rd,rh->dh", arrived, grad_pre, preferred_element_type=jnp.float32)
    grad_outer = jnp.einsum(
        "rh,rd->hd", hidden_act, grad_arrived, preferred_element_type=jnp.float32
    )
    grad_sent = jnp.dot(grad_pre, w_in[0].T, preferred_element_type=jnp.float32).astype(
        jnp.bfloat16
    )
    grad_w_in, grad_w_out = (
        lax.psum_scatter(
            grad_inner[None].astype(jnp.bfloat16), "seq", scatter_dimension=2, tiled=True
        ).astype(jnp.float32),
        lax.psum_scatter(
            grad_outer[None].astype(jnp.bfloat16), "seq", scatter_dimension=1, tiled=True
        ).astype(jnp.float32),
    )
    grad_back = lax.all_to_all(
        grad_sent.reshape(owners, slot_rows, model_width),
        "exp",
        split_axis=0,
        concat_axis=0,
        tiled=True,
    )
    grad_normed2 = grad_back.reshape(owners * slot_rows, model_width)[slot_index].astype(
        jnp.float32
    )
    norm_pull = jax.vjp(layer_norm, middle, norm_gain[:, 1], norm_bias[:, 1])[1]
    grad_mid_norm, grad_gain_two, grad_bias_two = norm_pull(grad_normed2)
    grad_middle = grad_out + grad_mid_norm
    grad_branch = grad_middle.astype(jnp.bfloat16)
    grad_attn_out = jnp.einsum(
        "rf,rd->fd", att_low, grad_branch, preferred_element_type=jnp.float32
    )
    grad_att = jnp.dot(grad_branch, full_out.T, preferred_element_type=jnp.float32).astype(
        jnp.bfloat16
    )
    grad_att = grad_att.reshape(seq_dev, rows_seq, head_count, head_dim)
    key_back, value_back = (key_full, value_full)
    probs_back = jnp.exp(scores_of(key_back) - log_total)
    key_heads = key_back.reshape(seq_dev, full_len, head_count, head_dim)
    value_back_heads = value_back.reshape(seq_dev, full_len, head_count, head_dim)
    grad_values = jnp.einsum(
        "shqk,sqhd->skhd",
        probs_back.astype(jnp.bfloat16),
        grad_att,
        preferred_element_type=jnp.float32,
    )
    grad_probs = jnp.einsum(
        "sqhd,skhd->shqk", grad_att, value_back_heads, preferred_element_type=jnp.float32
    )
    delta = jnp.sum(probs_back * grad_probs, axis=-1, keepdims=True)
    grad_scores = (probs_back * (grad_probs - delta)).astype(jnp.bfloat16)
    grad_query = (
        jnp.einsum("shqk,skhd->sqhd", grad_scores, key_heads, preferred_element_type=jnp.float32)
        * score_scale
    )
    grad_keys = (
        jnp.einsum("shqk,sqhd->skhd", grad_scores, queries, preferred_element_type=jnp.float32)
        * score_scale
    )
    grad_key_local, grad_value_local = (
        lax.psum_scatter(
            grad_keys.reshape(seq_dev, full_len, model_width).astype(jnp.bfloat16),
            "seq",
            scatter_dimension=1,
            tiled=True,
        ).astype(jnp.float32),
        lax.psum_scatter(
            grad_values.reshape(seq_dev, full_len, model_width).astype(jnp.bfloat16),
            "seq",
            scatter_dimension=1,
            tiled=True,
        ).astype(jnp.float32),
    )
    grad_qkv = jnp.concatenate(
        [
            grad_query.reshape(row_count, model_width).astype(jnp.bfloat16),
            grad_key_local.reshape(row_count, model_width).astype(jnp.bfloat16),
            grad_value_local.reshape(row_count, model_width).astype(jnp.bfloat16),
        ],
        axis=1,
    )
    grad_qkv_weight = jnp.einsum(
        "rd,re->de", normed_low, grad_qkv, preferred_element_type=jnp.float32
    )
    grad_normed = jnp.dot(grad_qkv, full_qkv.T, preferred_element_type=jnp.float32)
    first_pull = jax.vjp(layer_norm, tok_rows, norm_gain[:, 0], norm_bias[:, 0])[1]
    grad_rows_norm, grad_gain_one, grad_bias_one = first_pull(grad_normed)
    grad_tokens = (grad_middle + grad_rows_norm).reshape(seq_dev, rows_seq, model_width)
    grad_gain = jnp.stack([grad_gain_one, grad_gain_two], axis=1)
    grad_bias = jnp.stack([grad_bias_one, grad_bias_two], axis=1)
    grad_w_qkv, grad_w_attn_out, grad_norm_scale, grad_norm_shift = (
        lax.psum_scatter(grad_qkv_weight, ("exp", "seq"), scatter_dimension=0, tiled=True),
        lax.psum_scatter(grad_attn_out, ("exp", "seq"), scatter_dimension=0, tiled=True),
        lax.psum_scatter(grad_gain, ("exp", "seq"), scatter_dimension=0, tiled=True),
        lax.psum_scatter(grad_bias, ("exp", "seq"), scatter_dimension=0, tiled=True),
    )
    return (
        layer_out,
        grad_tokens,
        grad_w_qkv,
        grad_w_attn_out,
        grad_norm_scale,
        grad_norm_shift,
        grad_w_in,
        grad_w_out,
    )


def solution(mesh):
    return jax.shard_map(
        local,
        mesh=mesh,
        in_specs=(
            P("exp", "seq", None),
            P("exp", "seq", None),
            P("exp", "seq"),
            P("exp", None),
            P(),
            P(("exp", "seq"), None),
            P(("exp", "seq"), None),
            P(("exp", "seq"), None),
            P(("exp", "seq"), None),
            P("exp", None, None),
            P("exp", None, None),
        ),
        out_specs=(
            P("exp", "seq", None),
            P("exp", "seq", None),
            P(("exp", "seq"), None),
            P(("exp", "seq"), None),
            P(("exp", "seq"), None),
            P(("exp", "seq"), None),
            P("exp", None, "seq"),
            P("exp", "seq", None),
        ),
        check_vma=False,
    )
```

profile of v0, /device:TPU:0, one launch (start us, length us, event | category | flops | bytes accessed | tf_op | source)
XLA Modules:
  0.0 1051.3 jit_solution(5885426638870561313)
XLA Ops:
  11.4 69.5 %all-gather = bf16[32,24,2]{1,2,0:T(2,128)(2,1)S(1)} all-gather(bf16[1,24,2]{1,2,0:T(2,128)(2,1)} %bitcast.183), channel_id=1, replica_groups=mesh['exp'=8,'seq'=4] {'exp','seq'}, dimensions={0}, use_global_device_ids=true | all-gather | bytes 3168 | tf_op jit(solution)/shard_map/all_gather | solution.py:47
  81.0 63.2 %all-gather.1 = bf16[32,24,2]{1,2,0:T(2,128)(2,1)S(1)} all-gather(bf16[1,24,2]{1,2,0:T(2,128)(2,1)} %bitcast.184), channel_id=1, replica_groups=mesh['exp'=8,'seq'=4] {'exp','seq'}, dimensions={0}, use_global_device_ids=true | all-gather | bytes 3168 | tf_op jit(solution)/shard_map/all_gather | solution.py:48
  147.7 4.0 convolution_convert_fusion.2
  154.4 3.1 gather_fusion
  162.0 52.6 %all-gather.11.cloned.1.call-done = bf16[2,1024,768]{2,1,0:T(8,128)(2,1)} async-done(((bf16[2,256,768]{2,1,0:T(8,128)(2,1)}), bf16[2,1024,768]{2,1,0:T(8,128)(2,1)}) %all-gather.11.cloned.1.call-update) | async-done | bytes 3145744 | tf_op jit(solution)/shard_map/all_gather | solution.py:59
  214.6 3.2 copy.63
  217.8 13.1 %fusion.13 = (f32[2,12,256]{2,1,0:T(8,128)S(1)}, f32[2,12,256,1024]{3,2,1,0:T(8,128)}) fusion(pred[2,256,1024]{2,1,0:T(8,128)(4,1)} %compare_and_fusion, bf16[2,1024,12,64]{1,3,2,0:T(8,128)(2,1)S(1)} %bitcast.145, bf16[2,256,12,64]{1,0,3,2:T(2,128)(2,1)} %reshape.296), kind=kOutput, calls=%fused_computation.26 | convolution fusion | flops 824174592 | bytes 29646848 | tf_op jit(solution)/shard_map/sqhd,skhd->shqk/dot_general | solution.py:73
  231.0 11.8 %fusion = f32[2,12,256]{2,1,0:T(8,128)S(1)} fusion(f32[2,12,256]{2,1,0:T(8,128)S(1)} %get-tuple-element.29, f32[2,12,256,1024]{3,2,1,0:T(8,128)} %get-tuple-element.30, pred[2,256,1024]{2,1,0:T(8,128)(4,1)S(1)} %copy-done.11), kind=kLoop, calls=%fused_computation.13 | loop fusion | flops 25159680 | bytes 25739264 | tf_op jit(solution)/shard_map/reduce_sum | solution.py:81
  242.8 36.2 %all-gather.9.cloned.1.call-done = bf16[2,1024,768]{2,1,0:T(8,128)(2,1)} async-done(((bf16[2,256,768]{2,1,0:T(8,128)(2,1)}), bf16[2,1024,768]{2,1,0:T(8,128)(2,1)}) %all-gather.9.cloned.1.call-update) | async-done | bytes 3145744 | tf_op jit(solution)/shard_map/all_gather | solution.py:60
  279.0 4.6 copy.61
  283.6 12.7 %fusion.52 = bf16[2,256,12,64]{1,3,2,0:T(8,128)(2,1)S(1)} fusion(bf16[2,1024,12,64]{1,3,2,0:T(8,128)(2,1)} %bitcast.148, f32[2,12,256]{2,1,0:T(8,128)S(1)} %fusion, f32[2,12,256]{2,1,0:T(8,128)S(1)} %get-tuple-element.29, f32[2,12,256,1024]{3,2,1,0:T(8,128)} %get-tuple-element.30, pred[2,256,1024]{2,1,0:T(8,128)(4,1)S(1)} %copy-done.12), kind=kOutput, calls=%fused_computation.79 | convolution fusion | flops 837156864 | bytes 29671424 | tf_op jit(solution)/shard_map/shqk,skhd->sqhd/dot_general | solution.py:85
  298.2 36.2 %all-gather.13.cloned.1.call-done = bf16[768,768]{1,0:T(8,128)(2,1)} async-done(((bf16[24,768]{1,0:T(8,128)(2,1)}), bf16[768,768]{1,0:T(8,128)(2,1)}) %all-gather.13.cloned.1.call-update) | async-done | bytes 1179664 | tf_op jit(solution)/shard_map/all_gather | solution.py:46
  337.2 4.4 scatter_custom_fusion
  341.6 4.4 all-to-all-start
  346.0 4.8 scatter_custom_fusion.1
  350.8 24.7 %all-to-all-done = bf16[8,192,768]{2,1,0:T(8,128)(2,1)} async-done(((bf16[8,192,768]{2,1,0:T(8,128)(2,1)}), bf16[8,192,768]{2,1,0:T(8,128)(2,1)}, u32[]{:S(2)}, u32[]{:S(2)}) %all-to-all-start) | async-done | bytes 2359328 | tf_op jit(solution)/shard_map/all_to_all | solution.py:99
  375.5 3.8 all-to-all-start.2
  379.3 10.2 fusion.22
  389.5 6.4 copy-done.35
  395.9 14.4 %fusion.29 = bf16[1536,768]{1,0:T(8,128)(2,1)} fusion(bf16[1,3072,768]{2,1,0:T(8,128)(2,1)} %param.21, f32[1536,3072]{1,0:T(8,128)S(1)} %fusion.22), kind=kOutput, calls=%fused_computation.42 | convolution fusion | flops 7291404288 | bytes 25952256 | tf_op jit(solution)/shard_map/dot_general | solution.py:109
  411.7 4.4 all-to-all-start.1
  416.2 22.0 %fusion.8 = bf16[1536,3072]{1,0:T(8,128)(2,1)S(1)} fusion(f32[1536,3072]{1,0:T(8,128)} %copy-done.35, bf16[1536,768]{1,0:T(8,128)(2,1)} %bitcast.159, bf16[1,3072,768]{2,1,0:T(8,128)(2,1)} %param.21), kind=kOutput, calls=%fused_computation.21 | convolution fusion | flops 7342129152 | bytes 35389440 | tf_op jit(solution)/shard_map/dot_general | solution.py:135
  438.2 3.6 copy-done.34
  441.9 11.2 %fusion.26 = bf16[1536,768]{1,0:T(8,128)(2,1)} fusion(bf16[1536,3072]{1,0:T(8,128)(2,1)S(1)} %fusion.8, bf16[1,768,3072]{2,1,0:T(8,128)(2,1)} %param.20), kind=kOutput, calls=%fused_computation.41 | convolution fusion | flops 7248936960 | bytes 16515072 | tf_op jit(solution)/shard_map/dot_general | solution.py:141
  453.1 4.4 all-to-all-start.3
  457.5 3.2 gather_fusion.1
  460.7 26.2 %all-to-all-done.3 = bf16[8,192,768]{2,1,0:T(8,128)(2,1)} async-done(((bf16[8,192,768]{2,1,0:T(8,128)(2,1)}), bf16[8,192,768]{2,1,0:T(8,128)(2,1)}, u32[]{:S(2)}, u32[]{:S(2)}) %all-to-all-start.3) | async-done | bytes 2359328 | tf_op jit(solution)/shard_map/all_to_all | solution.py:152
  486.9 4.5 gather_fusion.2
  492.2 2.9 fusion.82
  498.6 12.4 %fusion.32 = bf16[2,12,64,1024]{3,2,1,0:T(8,128)(2,1)} fusion(f32[2,12,256]{2,1,0:T(8,128)S(1)} %log_add_fusion, f32[2,12,256,1024]{3,2,1,0:T(8,128)} %get-tuple-element.30, pred[2,256,1024]{2,1,0:T(8,128)(4,1)S(1)} %copy-done.12, bf16[2,256,12,64]{1,0,3,2:T(2,128)(2,1)S(1)} %reshape.311), kind=kOutput, calls=%fused_computation.49 | convolution fusion | flops 832045056 | bytes 29646848 | tf_op jit(solution)/shard_map/shqk,sqhd->skhd/dot_general | solution.py:177
  511.0 4.7 copy.72
  515.8 20.0 %multiply_reduce_fusion = (f32[2,12,256]{2,1,0:T(8,128)S(1)}, f32[2,12,256,1024]{3,2,1,0:T(8,128)}) fusion(f32[2,12,256]{2,1,0:T(8,128)S(1)} %log_add_fusion, f32[2,12,256,1024]{3,2,1,0:T(8,128)} %get-tuple-element.30, pred[2,256,1024]{2,1,0:T(8,128)(4,1)S(1)} %copy-done.12, bf16[2,1024,12,64]{1,3,2,0:T(8,128)(2,1)} %bitcast.149, ...), kind=kOutput, calls=%fused_computation.8 | convolution fusion | flops 836757504 | bytes 54837248 | tf_op jit(solution)/shard_map/sqhd,skhd->shqk/dot_general | solution.py:183
  535.8 17.1 %multiply_convert_fusion = bf16[2,12,256,1024]{3,2,1,0:T(8,128)(2,1)S(1)} fusion(f32[2,12,256,1024]{3,2,1,0:T(8,128)} %get-tuple-element.34, f32[2,12,256]{2,1,0:T(8,128)S(1)} %get-tuple-element.33, f32[2,12,256]{2,1,0:T(8,128)S(1)} %log_add_fusion, f32[2,12,256,1024]{3,2,1,0:T(8,128)} %get-tuple-element.30, pred[2,256,1024]{2,1,0:T(8,128)(4,1)S(1)} %copy-done.12), kind=kLoop, calls=%fused_computation.7 | loop fusion | flops 37748736 | bytes 63488000 | tf_op jit(solution)/shard_map/convert_element_type | solution.py:187
  562.0 15.8 %fusion.25 = bf16[1,3072,768]{2,1,0:T(8,128)(2,1)} fusion(bf16[1536,768]{1,0:T(8,128)(2,1)S(1)} %bitcast.160, f32[1536,3072]{1,0:T(8,128)} %copy-done.35), kind=kOutput, calls=%fused_computation.39 | convolution fusion | flops 7292583936 | bytes 25952256 | tf_op jit(solution)/shard_map/rh,rd->hd/dot_general | solution.py:138
  577.8 12.7 %fusion.24 = bf16[1,768,3072]{2,1,0:T(8,128)(2,1)} fusion(bf16[1536,768]{1,0:T(8,128)(2,1)} %bitcast.15, bf16[1536,3072]{1,0:T(8,128)(2,1)} %copy-done.34), kind=kOutput, calls=%fused_computation.38 | convolution fusion | flops 7250116608 | bytes 16515072 | tf_op jit(solution)/shard_map/rd,rh->dh/dot_general | solution.py:137
  590.6 3.8 fusion.85
  594.7 8.6 fusion.51
  605.7 31.0 %reduce-scatter.9.cloned.1.call-done = bf16[2,256,768]{2,1,0:T(8,128)(2,1)} async-done(((bf16[2,1024,768]{2,1,0:T(8,128)(2,1)}), bf16[2,256,768]{2,1,0:T(8,128)(2,1)}) %reduce-scatter.9.cloned.1.call-update) | async-done | bytes 786448 | tf_op jit(solution)/shard_map/reduce_scatter | solution.py:197
  638.2 5.0 fusion.58
  644.3 5.3 fusion.81
  651.7 44.1 %all-reduce.2 = (f32[768,2]{0,1:T(2,128)S(1)}, f32[768,2]{0,1:T(2,128)S(1)}) all-reduce(f32[768,2]{0,1:T(2,128)S(1)} %pad_maximum_fusion.3, f32[768,2]{0,1:T(2,128)S(1)} %pad_maximum_fusion.4), channel_id=6, replica_groups=mesh['exp'=8,'seq'=4] {'exp','seq'}, use_global_device_ids=true, to_apply=%region_22.23.clone | all-reduce | flops 3072 | bytes 24576
  696.4 3.4 add_add_fusion.2
  699.8 25.6 %reduce-scatter.19.cloned.1.call-done = bf16[1,768,768]{2,1,0:T(8,128)(2,1)} async-done(((bf16[1,3072,768]{2,1,0:T(8,128)(2,1)}), bf16[1,768,768]{2,1,0:T(8,128)(2,1)}) %reduce-scatter.19.cloned.1.call-update) | async-done | bytes 1179664 | tf_op jit(solution)/shard_map/reduce_scatter | solution.py:148
  725.4 2.8 convert_element_type.174
  728.2 85.2 %reduce-scatter.17.cloned.1.call-done = bf16[1,768,768]{2,1,0:T(8,128)(2,1)} async-done(((bf16[1,768,3072]{2,1,0:T(8,128)(2,1)}), bf16[1,768,768]{2,1,0:T(8,128)(2,1)}) %reduce-scatter.17.cloned.1.call-update) | async-done | bytes 1179664 | tf_op jit(solution)/shard_map/reduce_scatter | solution.py:145
  813.4 2.8 convert_element_type.171
  816.2 102.6 %reduce-scatter.15.cloned.1.call-done = f32[24,768]{1,0:T(8,128)} async-done(((f32[768,768]{1,0:T(8,128)}), f32[24,768]{1,0:T(8,128)}) %reduce-scatter.15.cloned.1.call-update) | async-done | bytes 73744 | tf_op jit(solution)/shard_map/reduce_scatter | solution.py:229
  918.8 125.3 %reduce-scatter.13.cloned.1.call-done = f32[24,2304]{1,0:T(8,128)} async-done(((f32[768,2304]{1,0:T(8,128)}), f32[24,2304]{1,0:T(8,128)}) %reduce-scatter.13.cloned.1.call-update) | async-done | bytes 221200 | tf_op jit(solution)/shard_map/reduce_scatter | solution.py:228
  (159 shorter events, 42.2 us)
Async XLA Ops:
  7.2 147.3 %copy-start = (s32[50257]{0:T(1024)S(1)}, s32[50257]{0:T(1024)}, u32[]{:S(2)}) copy-start(s32[50257]{0:T(1024)} %param.15) | copy-start | bytes 603088
  7.2 139.6 %all-gather.7.cloned.1.call-start = ((), (), s32[]{:S(2)}) async-start(), calls=%async_computation.10 | async-start | bytes 3649536 | tf_op jit(solution)/shard_map/all_gather | solution.py:45
  7.9 206.7 %all-gather.11.cloned.1.call-start = ((), (), s32[]{:S(2)}) async-start(), calls=%async_computation.12 | async-start | bytes 3932160 | tf_op jit(solution)/shard_map/all_gather | solution.py:59
  9.3 142.4 %copy-start.25 = (f32[1,2,2,128]{3,1,2,0:T(2,128)}, f32[1,2,2,128]{3,1,2,0:T(2,128)S(1)}, u32[]{:S(2)}) copy-start(f32[1,2,2,128]{3,1,2,0:T(2,128)S(1)} %copy.79) | copy-start | bytes 6148
  10.9 140.8 %copy-start.27 = (f32[512]{0:T(512)}, f32[512]{0:T(512)S(1)}, u32[]{:S(2)}) copy-start(f32[512]{0:T(512)S(1)} %rsqrt.22) | copy-start | bytes 6148
  146.8 0.9 copy-start.20
  151.7 2.7 copy-start.32
  153.0 6.3 copy-start.31
  153.0 125.9 %all-gather.9.cloned.1.call-start = ((), (), s32[]{:S(2)}) async-start(), calls=%async_computation.11 | async-start | bytes 3932160 | tf_op jit(solution)/shard_map/all_gather | solution.py:60
  153.8 180.7 %all-gather.13.cloned.1.call-start = ((), (), s32[]{:S(2)}) async-start(), calls=%async_computation.13 | async-start | bytes 1216512 | tf_op jit(solution)/shard_map/all_gather | solution.py:46
  217.8 13.2 %copy-start.3 = (bf16[2,1024,768]{1,2,0:T(8,128)(2,1)}, bf16[2,1024,768]{1,2,0:T(8,128)(2,1)S(1)}, u32[]{:S(2)}) copy-start(bf16[2,1024,768]{1,2,0:T(8,128)(2,1)S(1)} %copy.63) | copy-start | bytes 9437188
  217.8 13.2 %copy-start.11 = (pred[2,256,1024]{2,1,0:T(8,128)(4,1)S(1)}, pred[2,256,1024]{2,1,0:T(8,128)(4,1)}, u32[]{:S(2)}) copy-start(pred[2,256,1024]{2,1,0:T(8,128)(4,1)} %compare_and_fusion) | copy-start | bytes 1572868
  242.8 40.8 %copy-start.12 = (pred[2,256,1024]{2,1,0:T(8,128)(4,1)S(1)}, pred[2,256,1024]{2,1,0:T(8,128)(4,1)}, u32[]{:S(2)}) copy-start(pred[2,256,1024]{2,1,0:T(8,128)(4,1)} %compare_and_fusion) | copy-start | bytes 1572868
  296.3 38.2 %copy-start.7 = (bf16[2,256,768]{2,1,0:T(8,128)(2,1)S(1)}, bf16[2,256,768]{2,1,0:T(8,128)(2,1)}, u32[]{:S(2)}) copy-start(bf16[2,256,768]{2,1,0:T(8,128)(2,1)} %param.11) | copy-start | bytes 2359300
  336.9 4.8 copy-start.5
  341.6 33.8 %all-to-all-start = ((bf16[8,192,768]{2,1,0:T(8,128)(2,1)}), bf16[8,192,768]{2,1,0:T(8,128)(2,1)}, u32[]{:S(2)}, u32[]{:S(2)}) async-start(bf16[8,192,768]{2,1,0:T(8,128)(2,1)} %bitcast.150), calls=%async_computation | async-start | bytes 4718592 | tf_op jit(solution)/shard_map/all_to_all | solution.py:99
  375.5 34.9 %all-to-all-start.2 = ((bf16[8,192,768]{2,1,0:T(8,128)(2,1)}), bf16[8,192,768]{2,1,0:T(8,128)(2,1)S(1)}, u32[]{:S(2)}, u32[]{:S(2)}) async-start(bf16[8,192,768]{2,1,0:T(8,128)(2,1)} %bitcast.22), calls=%async_computation.2 | async-start | bytes 4718592 | tf_op jit(solution)/shard_map/all_to_all | solution.py:126
  389.5 6.4 copy-start.35
  410.3 1.4 copy-start.18
  411.7 41.3 %all-to-all-start.1 = ((bf16[8,192,768]{2,1,0:T(8,128)(2,1)}), bf16[8,192,768]{2,1,0:T(8,128)(2,1)S(1)}, u32[]{:S(2)}, u32[]{:S(2)}) async-start(bf16[8,192,768]{2,1,0:T(8,128)(2,1)} %bitcast.162), calls=%async_computation.1 | async-start | bytes 4718592 | tf_op jit(solution)/shard_map/all_to_all | solution.py:112
  438.2 3.6 copy-start.34
  453.1 33.8 %all-to-all-start.3 = ((bf16[8,192,768]{2,1,0:T(8,128)(2,1)}), bf16[8,192,768]{2,1,0:T(8,128)(2,1)}, u32[]{:S(2)}, u32[]{:S(2)}) async-start(bf16[8,192,768]{2,1,0:T(8,128)(2,1)} %bitcast.161), calls=%async_computation.3 | async-start | bytes 4718592 | tf_op jit(solution)/shard_map/all_to_all | solution.py:152
  457.5 146.8 %reduce-scatter.11.cloned.1.call-start = ((), (), s32[]{:S(2)}) async-start(), calls=%async_computation.15 | async-start | bytes 3932160 | tf_op jit(solution)/shard_map/reduce_scatter | solution.py:203
  486.9 4.5 copy-start.6
  492.1 4.1 copy-start.15
  492.2 5.2 copy-start.33
  495.1 1.1 copy-start.9
  496.5 0.9 copy-start.17
  515.7 121.0 %reduce-scatter.9.cloned.1.call-start = ((), (), s32[]{:S(2)}) async-start(), calls=%async_computation.14 | async-start | bytes 3932160 | tf_op jit(solution)/shard_map/reduce_scatter | solution.py:197
  535.8 17.1 %copy-start.13 = (bf16[2,256,12,64]{1,0,3,2:T(2,128)(2,1)S(1)}, bf16[2,256,12,64]{1,0,3,2:T(2,128)(2,1)}, u32[]{:S(2)}) copy-start(bf16[2,256,12,64]{1,0,3,2:T(2,128)(2,1)} %reshape.296) | copy-start | bytes 2359300
  552.9 4.6 copy-start.2
  560.3 1.7 copy-start.19
  560.3 165.1 %reduce-scatter.19.cloned.1.call-start = ((), (), s32[]{:S(2)}) async-start(), calls=%async_computation.19 | async-start | bytes 5898240 | tf_op jit(solution)/shard_map/reduce_scatter | solution.py:148
  577.8 235.6 %reduce-scatter.17.cloned.1.call-start = ((), (), s32[]{:S(2)}) async-start(), calls=%async_computation.18 | async-start | bytes 5898240 | tf_op jit(solution)/shard_map/reduce_scatter | solution.py:145
  590.5 4.2 copy-start.4
  590.5 328.3 %reduce-scatter.15.cloned.1.call-start = ((), (), s32[]{:S(2)}) async-start(), calls=%async_computation.17 | async-start | bytes 2433024 | tf_op jit(solution)/shard_map/reduce_scatter | solution.py:229
  594.4 449.8 %reduce-scatter.13.cloned.1.call-start = ((), (), s32[]{:S(2)}) async-start(), calls=%async_computation.16 | async-start | bytes 7299072 | tf_op jit(solution)/shard_map/reduce_scatter | solution.py:228
  603.3 34.9 %copy-start.21 = (bf16[512,768]{1,0:T(8,128)(2,1)S(1)}, bf16[512,768]{1,0:T(8,128)(2,1)}, u32[]{:S(2)}) copy-start(bf16[512,768]{1,0:T(8,128)(2,1)} %copy-done.20) | copy-start | bytes 2359300
  638.1 5.0 copy-start.22
  643.1 1.1 copy-start.8
  643.1 1.1 copy-start.24
  643.1 1.1 copy-start.26
  644.3 5.4 copy-start.30
  644.3 6.5 copy-start.28
  644.3 52.1 %copy-start.16 = (bf16[2,256,768]{2,1,0:T(8,128)(2,1)S(1)}, bf16[2,256,768]{2,1,0:T(8,128)(2,1)}, u32[]{:S(2)}) copy-start(bf16[2,256,768]{2,1,0:T(8,128)(2,1)} %param.12) | copy-start | bytes 2359300
  649.6 1.1 copy-start.14
  649.7 46.8 %copy-start.10 = (f32[512,768]{1,0:T(8,128)S(1)}, f32[512,768]{1,0:T(8,128)}, u32[]{:S(2)}) copy-start(f32[512,768]{1,0:T(8,128)} %copy-done.9) | copy-start | bytes 4718596
  696.4 347.7 %copy-start.1 = (s32[50257]{0:T(1024)S(1)}, s32[50257]{0:T(1024)}, u32[]{:S(2)}) copy-start(s32[50257]{0:T(1024)} %param.15) | copy-start | bytes 603088
  (2 other events, 1.1 us)
Sparse Core Ops, SparseCore 0:
  10.8 62.8 all-gather.6
  153.2 61.4 all-gather.10
  216.8 62.1 all-gather.8
  281.6 52.7 all-gather.12
  515.8 58.3 reduce-scatter.10
  576.4 60.2 reduce-scatter.8
  639.0 86.3 reduce-scatter.18
  727.7 85.6 reduce-scatter.16
  819.3 99.5 reduce-scatter.14
  925.9 118.2 reduce-scatter.12
where the time goes:
time: 1060 us; the launch traced here: 1050 us
  waiting for transfers between devices  547 us (52%)
  blocking collectives  177 us (17%)
  matrix products  177 us (17%)
  local copies, waits for them, and re-layouts  62.8 us (6%)
  other arithmetic  54.5 us (5%)
  starting transfers between devices  18.2 us (2%)
  between operations  15.1 us (1%)
    reduce_scatter x1, waiting for transfers between devices, local(): lax.psum_scatter(grad_qkv_weight, ('exp', 'seq'), scatter_dimension=0, ti...  125 us
    reduce_scatter x1, waiting for transfers between devices, local(): lax.psum_scatter(grad_attn_out, ('exp', 'seq'), scatter_dimension=0, tile...  103 us
    reduce_scatter x1, waiting for transfers between devices, local(): lax.psum_scatter(grad_inner[None].astype(jnp.bfloat16), 'seq', scatter_di...  85.2 us
    all_gather x1, blocking collectives, local(): lax.all_gather(norm_scale, ('exp', 'seq'), axis=0, tiled=True)  69.5 us
    all_gather x1, blocking collectives, local(): lax.all_gather(norm_shift, ('exp', 'seq'), axis=0, tiled=True)  63.2 us
    all_gather x1, waiting for transfers between devices, local(): lax.all_gather(key_local, 'seq', axis=1, tiled=True)  52.6 us
    unnamed x1, blocking collectives  44.1 us
    all_gather x1, waiting for transfers between devices, local(): lax.all_gather(w_attn_out, ('exp', 'seq'), axis=0, tiled=True)  36.2 us
  transfers between devices with their start and end apart: 14, of which 10 were waited for; matrix products, arithmetic and copies ran while one was open for 22% of the time, Pallas kernels for 0%

commit v1 on v0

v1 whole, which is shorter than its diff:
```python
import functools

import jax
import jax.numpy as jnp
from jax import lax
from jax.experimental import pallas as pl
from jax.experimental.pallas import tpu as pltpu
from jax.sharding import PartitionSpec as P

HEAD_DIM = 64
LANES = 128
BOTH = ("exp", "seq")
epsilon = 1e-05
f32 = jnp.float32
bf16 = jnp.bfloat16


def gelu_tanh(feature):
    return jax.nn.gelu(feature, approximate=True)


def norm_parts(feature):
    center = feature - jnp.mean(feature, axis=-1, keepdims=True)
    spread = jnp.mean(center * center, axis=-1, keepdims=True)
    rstd = lax.rsqrt(spread + epsilon)
    return center * rstd, rstd


def norm_pull(grad_hat, hat, rstd):
    first = jnp.mean(grad_hat, axis=-1, keepdims=True)
    second = jnp.mean(grad_hat * hat, axis=-1, keepdims=True)
    return rstd * (grad_hat - first - hat * second)


def pick(array, index, axis=0):
    return lax.dynamic_index_in_dim(array, index, axis, keepdims=False)


def order_by_xor(parts, index):
    bit = 0
    while (1 << bit) < len(parts):
        flag = ((index >> bit) & 1) == 1
        parts = [
            jnp.where(flag, parts[place ^ (1 << bit)], parts[place]) for place in range(len(parts))
        ]
        bit += 1
    return parts


def nt(a, b):
    return lax.dot_general(a, b, (((1,), (1,)), ((), ())), preferred_element_type=f32)


def nn(a, b):
    return lax.dot_general(a, b, (((1,), (0,)), ((), ())), preferred_element_type=f32)


def tn(a, b):
    return lax.dot_general(a, b, (((0,), (0,)), ((), ())), preferred_element_type=f32)


def allowed_keys(segc_ref, segr_ref, start, block):
    width = start + block
    keys = lax.broadcasted_iota(jnp.int32, (width, block), 0)
    queries = lax.broadcasted_iota(jnp.int32, (width, block), 1) + start
    same = segc_ref[0:width, :] == segr_ref[:, start : start + block]
    return same & (keys <= queries)


def attend_kernel(q_ref, k_ref, v_ref, segc_ref, segr_ref, att_ref, lse_ref, *, block):
    total = q_ref.shape[0]
    values_t = v_ref[...].astype(f32).T.astype(bf16)
    lane = lax.broadcasted_iota(jnp.int32, (block, LANES), 1)
    for start in range(0, total, block):
        width = start + block
        allowed = allowed_keys(segc_ref, segr_ref, start, block)
        queries = q_ref[start:width, :] * 0.125
        outs = []
        for head in range(2):
            own = (lane >= HEAD_DIM) if head else (lane < HEAD_DIM)
            q_head = jnp.where(own, queries, 0.0).astype(bf16)
            scores = jnp.where(allowed, nt(k_ref[0:width, :], q_head), -1e30)
            top = jnp.max(scores, axis=0, keepdims=True)
            expo = jnp.exp(scores - top)
            total_row = jnp.sum(expo, axis=0, keepdims=True)
            out = nn(values_t[head * HEAD_DIM : (head + 1) * HEAD_DIM, 0:width], expo.astype(bf16))
            outs.append(out / total_row)
            lse_ref[0, head : head + 1, start:width] = top + jnp.log(total_row)
        att_ref[start:width, :] = jnp.concatenate(outs, axis=0).T.astype(bf16)


def attend(qkv, seg_col, seg_row):
    total, width = qkv.shape
    pairs = width // 3 // LANES
    block = min(256, total)
    column = lambda part: pl.BlockSpec((total, LANES), lambda h: (0, part * pairs + h))
    return pl.pallas_call(
        functools.partial(attend_kernel, block=block),
        grid=(pairs,),
        in_specs=[
            column(0),
            column(1),
            column(2),
            pl.BlockSpec((total, 1), lambda h: (0, 0)),
            pl.BlockSpec((1, total), lambda h: (0, 0)),
        ],
        out_specs=[
            pl.BlockSpec((total, LANES), lambda h: (0, h)),
            pl.BlockSpec((1, 8, total), lambda h: (h, 0, 0)),
        ],
        out_shape=[
            jax.ShapeDtypeStruct((total, pairs * LANES), bf16),
            jax.ShapeDtypeStruct((pairs, 8, total), f32),
        ],
        compiler_params=pltpu.CompilerParams(vmem_limit_bytes=48 << 20),
        cost_estimate=pl.CostEstimate(
            flops=4 * total * total * width // 6,
            bytes_accessed=2 * total * width * 2,
            transcendentals=total * total * width // 3 // HEAD_DIM // 2,
        ),
        name="attend",
    )(qkv, qkv, qkv, seg_col, seg_row)


def attend_back_kernel(
    q_ref,
    k_ref,
    v_ref,
    att_ref,
    datt_ref,
    lse_ref,
    segc_ref,
    segr_ref,
    out_ref,
    dk_ref,
    dv_ref,
    *,
    block,
):
    total = q_ref.shape[0]
    pairs = pl.num_programs(0)
    pair = pl.program_id(0)
    lane = lax.broadcasted_iota(jnp.int32, (block, LANES), 1)
    lane_all = lax.broadcasted_iota(jnp.int32, (total, LANES), 1)
    dk_ref[...] = jnp.zeros_like(dk_ref)
    dv_ref[...] = jnp.zeros_like(dv_ref)
    row8 = lax.broadcasted_iota(jnp.int32, (8, LANES), 0)
    lane8 = lax.broadcasted_iota(jnp.int32, (8, LANES), 1)
    head_rows = jnp.where(row8 == lane8 // HEAD_DIM, 1.0, 0.0)

    def column(part):
        return pl.ds(pl.multiple_of((part * pairs + pair) * LANES, LANES), LANES)

    for start in range(0, total, block):
        width = start + block
        allowed = allowed_keys(segc_ref, segr_ref, start, block)
        queries = q_ref[start:width, :] * 0.125
        grads = datt_ref[start:width, :]
        product = grads.astype(f32) * att_ref[start:width, :].astype(f32)
        delta = lax.dot_general(
            head_rows,
            product,
            (((1,), (1,)), ((), ())),
            precision=lax.Precision.HIGHEST,
            preferred_element_type=f32,
        )
        dq = jnp.zeros((block, LANES), f32)
        for head in range(2):
            own = (lane >= HEAD_DIM) if head else (lane < HEAD_DIM)
            own_all = (lane_all >= HEAD_DIM) if head else (lane_all < HEAD_DIM)
            q_head = jnp.where(own, queries, 0.0).astype(bf16)
            g_head = jnp.where(own, grads, 0.0).astype(bf16)
            k_head = jnp.where(own_all[0:width], k_ref[0:width, :], 0.0).astype(bf16)
            scores = nt(k_ref[0:width, :], q_head)
            probs = jnp.where(allowed, jnp.exp(scores - lse_ref[0, head : head + 1, start:width]), 0.0)
            dprobs = nt(v_ref[0:width, :], g_head)
            dscores = (probs * (dprobs - delta[head : head + 1, :])).astype(bf16)
            dv_ref[0:width, :] += nn(probs.astype(bf16), g_head)
            dk_ref[0:width, :] += nn(dscores, q_head)
            dq = dq + tn(dscores, k_head)
        out_ref[start:width, column(0)] = (dq * 0.125).astype(bf16)
    out_ref[:, column(1)] = dk_ref[...].astype(bf16)
    out_ref[:, column(2)] = dv_ref[...].astype(bf16)


def attend_back(qkv, att, datt, lse, seg_col, seg_row):
    total, width = qkv.shape
    pairs = width // 3 // LANES
    block = min(256, total)
    column = lambda part: pl.BlockSpec((total, LANES), lambda h: (0, part * pairs + h))
    return pl.pallas_call(
        functools.partial(attend_back_kernel, block=block),
        grid=(pairs,),
        in_specs=[
            column(0),
            column(1),
            column(2),
            column(0),
            column(0),
            pl.BlockSpec((1, 8, total), lambda h: (h, 0, 0)),
            pl.BlockSpec((total, 1), lambda h: (0, 0)),
            pl.BlockSpec((1, total), lambda h: (0, 0)),
        ],
        out_specs=pl.BlockSpec((total, width), lambda h: (0, 0)),
        out_shape=jax.ShapeDtypeStruct((total, width), bf16),
        scratch_shapes=[pltpu.VMEM((total, LANES), f32), pltpu.VMEM((total, LANES), f32)],
        compiler_params=pltpu.CompilerParams(vmem_limit_bytes=48 << 20),
        cost_estimate=pl.CostEstimate(
            flops=10 * total * total * width // 6,
            bytes_accessed=3 * total * width * 2,
            transcendentals=total * total * width // 3 // HEAD_DIM // 2,
        ),
        name="attend_back",
    )(qkv, qkv, qkv, att, datt, lse, seg_col, seg_row)


def make_local(exp_size, seq_size):
    cols = exp_size // 2
    col_bits = cols.bit_length() - 1

    def flat_perm(target):
        pairs = []
        for exp in range(exp_size):
            for seq in range(seq_size):
                col, core = exp >> 1, exp & 1
                new_col, new_core, new_seq = target(col, core, seq)
                pairs.append((exp * seq_size + seq, (new_col * 2 + new_core) * seq_size + new_seq))
        return pairs

    def send(array, target):
        return lax.ppermute(array, BOTH, flat_perm(target))

    def to_core(array):
        return send(array, lambda c, k, z: (c, 1 - k, z))

    def to_seq(array, shift):
        return send(array, lambda c, k, z: (c, k, z ^ shift))

    def to_col(array, bit):
        return send(array, lambda c, k, z: (c ^ (1 << bit), k, z))

    def home_of(i):
        return lambda c, k, z: (c, z >> 1, (2 * k + (z & 1)) ^ i)

    def worker_of(i):
        return lambda c, k, z: (c, (z ^ i) >> 1, 2 * k + ((z ^ i) & 1))

    def local(
        tokens,
        cotangent,
        token_ids,
        segments,
        hash_table,
        w_qkv,
        w_attn_out,
        norm_scale,
        norm_shift,
        w_in,
        w_out,
    ):
        seq_dev, rows_seq, width = tokens.shape
        rows = seq_dev * rows_seq
        slot_rows = 3 * rows // exp_size
        full_len = rows_seq * seq_size
        half = width // 2
        part_rows = w_qkv.shape[0]
        exp_at = lax.axis_index("exp")
        z = lax.axis_index("seq")
        k = exp_at & 1
        c = exp_at >> 1

        norms = jnp.concatenate([norm_scale, norm_shift], axis=1)
        norms = jnp.pad(norms, ((0, 0), (0, LANES - norms.shape[1])))
        qkv_parts = w_qkv.reshape(part_rows, 3, 2, half)
        packs = [
            jnp.concatenate(
                [qkv_parts[:, i, core] for i in range(3)]
                + [w_attn_out[:, core * half : (core + 1) * half], norms],
                axis=1,
            )
            for core in range(2)
        ]
        is_one = k == 1
        keep = jnp.where(is_one, packs[1], packs[0])
        away = to_core(jnp.where(is_one, packs[0], packs[1]))
        pair = jnp.stack([jnp.where(is_one, away, keep), jnp.where(is_one, keep, away)])
        got = [pair] + [to_seq(pair, i) for i in range(1, seq_size)]
        gathered = jnp.stack(order_by_xor(got, z), axis=1)
        wide = gathered.shape[-1]
        halves = []
        for kk in range(2):
            block = gathered[kk]
            bits = list(range(col_bits))
            if kk:
                bits = bits[::-1]
            done = []
            for bit in bits:
                other = to_col(block, bit)
                flag = ((c >> bit) & 1) == 1
                place = sum(1 for b in done if b > bit)
                block = jnp.stack(
                    [jnp.where(flag, other, block), jnp.where(flag, block, other)], axis=place
                )
                done.append(bit)
            halves.append(block.reshape(cols, seq_size * part_rows, wide))
        weights = jnp.stack(halves, axis=1).reshape(width, wide)
        wq = weights[:, : 3 * half]
        wo_own = weights[:, 3 * half : 4 * half]
        wo_other = to_core(wo_own)
        wo = jnp.concatenate(
            [jnp.where(is_one, wo_other, wo_own), jnp.where(is_one, wo_own, wo_other)], axis=1
        )
        norm_rows = weights[:, 4 * half : 4 * half + 4].astype(f32).T
        gain_one, gain_two, bias_one, bias_two = (norm_rows[i : i + 1] for i in range(4))

        z0 = z & 1
        here_a = send(pick(tokens, z0), home_of(0))
        here_b = send(pick(tokens, 1 - z0), home_of(1))
        flip = z0 == 1
        x_half = jnp.concatenate(
            [jnp.where(flip, here_b, here_a), jnp.where(flip, here_a, here_b)], axis=0
        )
        x_other = to_core(x_half)
        x_seq = jnp.concatenate(
            [jnp.where(is_one, x_other, x_half), jnp.where(is_one, x_half, x_other)], axis=0
        )
        seg_other = to_core(segments)
        seg_pair = jnp.where((z >> 1) == k, segments, seg_other)
        seg_row = pick(seg_pair, z0)[None, :]
        seg_col = seg_row.reshape(full_len, 1)

        expert = hash_table[token_ids.reshape(-1)]
        order = jnp.arange(rows, dtype=jnp.int32)
        earlier = (expert[None, :] == expert[:, None]) & (order[None, :] < order[:, None])
        slot_rank = jnp.sum(earlier.astype(jnp.int32), axis=1)
        slot_index = expert * slot_rows + slot_rank
        slots = exp_size * slot_rows
        spread = (jnp.arange(slots, dtype=jnp.int32)[:, None] == slot_index[None, :]).astype(bf16)

        def swap(array):
            return lax.all_to_all(
                array.reshape(exp_size, slot_rows, width),
                "exp",
                split_axis=0,
                concat_axis=0,
                tiled=True,
            ).reshape(slots, width)

        grad_low = cotangent.reshape(rows, width)
        grad_arrived = swap(nn(spread, grad_low).astype(bf16))

        hat_seq, _ = norm_parts(x_seq.astype(f32))
        normed = (hat_seq * gain_one + bias_one).astype(bf16)
        qkv = nn(normed, wq).astype(bf16)
        att, lse = attend(qkv, seg_col, seg_row)

        chunk_at = 2 * k + z0
        att_chunks = att.reshape(seq_size, rows_seq, half)
        came = [send(pick(att_chunks, chunk_at ^ i), home_of(i)) for i in range(4)]
        quads = order_by_xor(came, z)
        att_home = jnp.concatenate(
            [
                jnp.concatenate([quads[0], quads[2]], axis=1),
                jnp.concatenate([quads[1], quads[3]], axis=1),
            ],
            axis=0,
        )
        tok_rows = tokens.reshape(rows, width).astype(f32)
        middle = tok_rows + nn(att_home, wo)
        hat_two, rstd_two = norm_parts(middle)
        sent = (hat_two * gain_two + bias_two).astype(bf16)

        arrived = swap(nn(spread, sent).astype(bf16))
        hidden_pre = nn(arrived, w_in[0])
        hidden_act = gelu_tanh(hidden_pre).astype(bf16)
        grad_outer = tn(hidden_act, grad_arrived).astype(bf16)
        grad_w_out = lax.psum_scatter(grad_outer, "seq", scatter_dimension=0, tiled=True)
        grad_act = nt(grad_arrived, w_out[0])
        grad_pre = jax.vjp(gelu_tanh, hidden_pre)[1](grad_act)[0].astype(bf16)
        grad_sent = nt(grad_pre, w_in[0]).astype(bf16)
        grad_back = swap(grad_sent)
        grad_inner = tn(arrived, grad_pre).astype(bf16)
        grad_w_in = lax.psum_scatter(grad_inner, "seq", scatter_dimension=1, tiled=True)
        returned = swap(nn(hidden_act, w_out[0]).astype(bf16))
        layer_out = (middle + tn(spread, returned)).astype(bf16)

        grad_normed2 = tn(spread, grad_back)
        grad_middle = grad_low.astype(f32) + norm_pull(grad_normed2 * gain_two, hat_two, rstd_two)
        grad_gain_two = jnp.sum(grad_normed2 * hat_two, axis=0, keepdims=True)
        grad_bias_two = jnp.sum(grad_normed2, axis=0, keepdims=True)
        grad_branch = grad_middle.astype(bf16)
        grad_att = nt(grad_branch, wo).astype(bf16)

        quads = grad_att.reshape(seq_dev, rows_seq, 2, half)
        quads = jnp.stack([quads[:, :, 0], quads[:, :, 1]]).reshape(4, rows_seq, half)
        came = [send(pick(quads, z ^ i), worker_of(i)) for i in range(4)]
        datt = jnp.concatenate(order_by_xor(came, chunk_at), axis=0)
        dqkv = attend_back(qkv, att, datt, lse, seg_col, seg_row)
        partial = nt(dqkv, wq)
        partial = partial.reshape(2, rows, width)
        grad_normed = pick(partial, k) + to_core(pick(partial, 1 - k).astype(bf16)).astype(f32)
        hat_half = pick(hat_seq.reshape(2, rows, width), k)
        grad_gain_one = jnp.sum(grad_normed * hat_half, axis=0, keepdims=True)
        grad_bias_one = jnp.sum(grad_normed, axis=0, keepdims=True)
        back = grad_normed.astype(bf16).reshape(2, rows_seq, width)
        back_a = send(pick(back, z0), home_of(0))
        back_b = send(pick(back, 1 - z0), home_of(1))
        normed_home = jnp.concatenate(
            [jnp.where(flip, back_b, back_a), jnp.where(flip, back_a, back_b)], axis=0
        ).astype(f32)
        hat_one, rstd_one = norm_parts(tok_rows)
        grad_tokens = grad_middle + norm_pull(normed_home * gain_one, hat_one, rstd_one)

        grad_wo = tn(att_home, grad_branch).reshape(width, 2, half)
        grad_wo = pick(grad_wo, k, 1) + to_core(pick(grad_wo, 1 - k, 1).astype(bf16)).astype(f32)
        grad_wq = tn(normed, dqkv)
        small = jnp.concatenate([grad_gain_one, grad_gain_two, grad_bias_one, grad_bias_two], axis=0)
        small = jnp.pad(small, ((0, LANES - 4), (0, 0))).T
        whole = jnp.concatenate([grad_wq, grad_wo, small], axis=1)
        whole = whole.reshape(cols, 2, seq_size * part_rows, wide)
        sums = []
        for kk in range(2):
            block = whole[:, kk].reshape((2,) * col_bits + (seq_size * part_rows, wide))
            bits = list(range(col_bits))
            if kk:
                bits = bits[::-1]
            left = list(range(col_bits))[::-1]
            for bit in bits:
                axis = left.index(bit)
                own_bit = (c >> bit) & 1
                away = to_col(pick(block, 1 - own_bit, axis).astype(bf16), bit)
                block = pick(block, own_bit, axis) + away.astype(f32)
                left.remove(bit)
            sums.append(block)
        own = jnp.where(is_one, sums[1], sums[0])
        away = to_core(jnp.where(is_one, sums[0], sums[1]).astype(bf16)).astype(f32)
        merged = [
            jnp.where(is_one, away, own)[:, : 4 * half],
            jnp.where(is_one, own, away)[:, : 4 * half],
            (own + away)[:, 4 * half :],
        ]
        merged = jnp.concatenate(merged, axis=1).reshape(seq_size, part_rows, 8 * half + LANES)
        final = pick(merged, z)
        for i in range(1, seq_size):
            final = final + to_seq(pick(merged, z ^ i).astype(bf16), i).astype(f32)
        pieces = [final[:, i * half : (i + 1) * half] for i in range(8)]
        grad_w_qkv = jnp.concatenate([pieces[i] for i in (0, 4, 1, 5, 2, 6)], axis=1)
        grad_w_attn_out = jnp.concatenate([pieces[3], pieces[7]], axis=1)
        grad_norms = final[:, 8 * half : 8 * half + 4]
        return (
            layer_out.reshape(seq_dev, rows_seq, width),
            grad_tokens.reshape(seq_dev, rows_seq, width),
            grad_w_qkv,
            grad_w_attn_out,
            grad_norms[:, 0:2],
            grad_norms[:, 2:4],
            grad_w_in.astype(f32)[None],
            grad_w_out.astype(f32)[None],
        )

    return local


def solution(mesh):
    return jax.shard_map(
        make_local(mesh.shape["exp"], mesh.shape["seq"]),
        mesh=mesh,
        in_specs=(
            P("exp", "seq", None),
            P("exp", "seq", None),
            P("exp", "seq"),
            P("exp", None),
            P(),
            P(("exp", "seq"), None),
            P(("exp", "seq"), None),
            P(("exp", "seq"), None),
            P(("exp", "seq"), None),
            P("exp", None, None),
            P("exp", None, None),
        ),
        out_specs=(
            P("exp", "seq", None),
            P("exp", "seq", None),
            P(("exp", "seq"), None),
            P(("exp", "seq"), None),
            P(("exp", "seq"), None),
            P(("exp", "seq"), None),
            P("exp", None, "seq"),
            P("exp", "seq", None),
        ),
        check_vma=False,
    )
```

time: 1060 us -> 472 us (0.45)
  waiting for transfers between devices: 547 us -> 150 us
  blocking collectives: 177 us -> 0 us
  starting transfers between devices: 18.2 us -> 95.9 us
  matrix products: 177 us -> 124 us
  local copies, waits for them, and re-layouts: 62.8 us -> 27.1 us
  other arithmetic: 54.5 us -> 22.4 us
  Pallas kernels: 0 us -> 27.4 us
    reduce_scatter x6 -> x2, waiting for transfers between devices: 370 us -> 0.01 us  [the longest x1 0.01 us: local(): lax.psum_scatter(grad_inner, 'seq', scatter_dimension=1, tiled=True)]
    all_gather x2 -> x0, blocking collectives: 133 us -> none  [the longest x1 69.5 us: local(): lax.all_gather(norm_scale, ('exp', 'seq'), axis=0, tiled=True)]
    all_gather x4 -> x0, waiting for transfers between devices: 125 us -> none  [the longest x1 52.6 us: local(): lax.all_gather(key_local, 'seq', axis=1, tiled=True)]
    ppermute x0 -> x33, waiting for transfers between devices: none -> 91.8 us  [send(): return lax.ppermute(array, BOTH, flat_perm(target))]
    ppermute x0 -> x33, starting transfers between devices: none -> 74.2 us  [send(): return lax.ppermute(array, BOTH, flat_perm(target))]
    dot_general x18 -> x16, matrix products: 177 us -> 124 us  [the longest x6 42.8 us: tn(): lax.dot_general(a, b, (((0,), (0,)), ((), ())), preferred_element_type=f32)]
    unnamed x1 -> x0, blocking collectives: 44.1 us -> none
    pallas_call x0 -> x2, Pallas kernels: none -> 27.4 us  [the longest x1 14.9 us: attend_back(): pl.pallas_call(functools.partial(attend_back_kernel, block=block), grid=(...]
  transfers between devices with their start and end apart: 14 -> 39, of which waited for: 10 -> 21; matrix products, arithmetic and copies ran while one was open for 22% -> 27% of each run, Pallas kernels for 0% -> 6%
where the time goes in v1:
time: 472 us; the launch traced here: 463 us
  waiting for transfers between devices  150 us (32%)
  matrix products  124 us (26%)
  starting transfers between devices  95.9 us (20%)
  Pallas kernels  27.4 us (6%)
  local copies, waits for them, and re-layouts  27.1 us (6%)
  other arithmetic  22.4 us (5%)
  between operations  15.7 us (3%)
    ppermute x33, waiting for transfers between devices, send(): return lax.ppermute(array, BOTH, flat_perm(target))  91.8 us
    ppermute x33, starting transfers between devices, send(): return lax.ppermute(array, BOTH, flat_perm(target))  74.2 us
    all_to_all x4, waiting for transfers between devices, swap(): lax.all_to_all(array.reshape(exp_size, slot_rows, width), 'exp', split_ax...  58.4 us
    dot_general x6, matrix products, tn(): lax.dot_general(a, b, (((0,), (0,)), ((), ())), preferred_element_type=f32)  42.8 us
    dot_general x6, matrix products, nn(): lax.dot_general(a, b, (((1,), (0,)), ((), ())), preferred_element_type=f32)  41.4 us
    dot_general x4, matrix products, nt(): lax.dot_general(a, b, (((1,), (1,)), ((), ())), preferred_element_type=f32)  39.8 us
    all_to_all x4, starting transfers between devices, swap(): lax.all_to_all(array.reshape(exp_size, slot_rows, width), 'exp', split_ax...  21.7 us
    pallas_call x1, Pallas kernels, attend_back(): pl.pallas_call(functools.partial(attend_back_kernel, block=block), grid=(...  14.9 us
  transfers between devices with their start and end apart: 39, of which 21 were waited for; matrix products, arithmetic and copies ran while one was open for 27% of the time, Pallas kernels for 6%

profile of v1, /device:TPU:0, one launch (start us, length us, event | category | flops | bytes accessed | tf_op | source)
XLA Modules:
  0.0 462.8 jit_solution(2158147782328453778)
XLA Ops:
  11.7 2.7 collective-permute-start
  16.5 3.1 gather_fusion
  20.8 3.4 collective-permute-start.6
  25.4 4.4 collective-permute-done.4
  29.9 13.9 %collective-permute-done.5 = bf16[2,24,1664]{2,1,0:T(8,128)(2,1)S(1)} collective-permute-done((bf16[2,24,1664]{2,1,0:T(8,128)(2,1)S(1)}, bf16[2,24,1664]{2,1,0:T(8,128)(2,1)S(1)}, u32[]{:S(2)}, u32[]{:S(2)}) %collective-permute-start.5) | collective-permute-done | bytes 159776 | tf_op jit(solution)/shard_map/ppermute | solution.py:231
  48.0 3.4 collective-permute-done.7
  56.4 9.7 %collective-permute-done.10 = bf16[2,4,24,1664]{3,2,1,0:T(8,128)(2,1)S(1)} collective-permute-done((bf16[2,4,24,1664]{3,2,1,0:T(8,128)(2,1)S(1)}, bf16[2,4,24,1664]{3,2,1,0:T(8,128)(2,1)S(1)}, u32[]{:S(2)}, u32[]{:S(2)}) %collective-permute-start.10) | collective-permute-done | bytes 639008 | tf_op jit(solution)/shard_map/ppermute | solution.py:231
  68.9 3.7 convolution_convert_fusion.2.q_ref.k_ref.v_ref
  72.6 12.5 %attend.1 = (bf16[1024,384]{1,0:T(8,128)(2,1)S(1)}, f32[3,8,1024]{2,1,0:T(8,128)S(1)}) custom-call(bf16[1024,1152]{1,0:T(8,128)(2,1)S(1)} %convolution_convert_fusion.2.q_ref.k_ref.v_ref, bf16[1024,1152]{1,0:T(8,128)(2,1)S(1)} %convolution_convert_fusion.2.q_ref.k_ref.v_ref, bf16[1024,1152]{1,0:T(8,128)(2,1)S(1)} %convolution_convert_fusion.2.q_ref.k_ref.v_ref, ...), custom_call_target="tpu_custom_call" | custom-call | flops 805306368 | bytes 4718592 | tf_op jit(solution)/shard_map/attend/pallas_call | solution.py:97
  85.3 5.9 %collective-permute-start.12 = (bf16[256,384]{1,0:T(8,128)(2,1)S(1)}, bf16[256,384]{1,0:T(8,128)(2,1)S(1)}, u32[]{:S(2)}, u32[]{:S(2)}) collective-permute-start(bf16[256,384]{1,0:T(8,128)(2,1)S(1)} %get-tuple-element.145), channel_id=1, source_target_pairs={{0,3},{1,2},{2,7},{3,6},{4,1},{5,0},{6,5},{7,4},{8,11},{9,10},{10,... | collective-permute-start | bytes 589832 | tf_op jit(solution)/shard_map/ppermute | solution.py:231
  92.8 3.7 collective-permute-done.12
  96.5 4.2 collective-permute-done.13
  104.5 3.2 convolution_convert_fusion.4
  107.7 8.5 %all-to-all-start = ((bf16[8,192,768]{2,1,0:T(8,128)(2,1)}), bf16[8,192,768]{2,1,0:T(8,128)(2,1)}, u32[]{:S(2)}, u32[]{:S(2)}) async-start(bf16[8,192,768]{2,1,0:T(8,128)(2,1)} %bitcast.256), calls=%async_computation | async-start | bytes 4718592 | tf_op jit(solution)/shard_map/all_to_all | solution.py:341
  116.2 2.9 convolution_convert_fusion.3
  119.1 27.0 %all-to-all-done = bf16[8,192,768]{2,1,0:T(8,128)(2,1)} async-done(((bf16[8,192,768]{2,1,0:T(8,128)(2,1)}), bf16[8,192,768]{2,1,0:T(8,128)(2,1)}, u32[]{:S(2)}, u32[]{:S(2)}) %all-to-all-start) | async-done | bytes 2359328 | tf_op jit(solution)/shard_map/all_to_all | solution.py:341
  146.1 4.4 all-to-all-start.2
  150.5 13.7 %fusion.15 = f32[1536,3072]{1,0:T(8,128)} fusion(bf16[1536,768]{1,0:T(8,128)(2,1)} %bitcast.31, bf16[1,768,3072]{2,1,0:T(8,128)(2,1)} %param.20), kind=kOutput, calls=%fused_computation.20 | convolution fusion | flops 7247757312 | bytes 25952256 | tf_op jit(solution)/shard_map/dot_general | solution.py:55
  164.2 15.7 %all-to-all-done.2 = bf16[8,192,768]{2,1,0:T(8,128)(2,1)} async-done(((bf16[8,192,768]{2,1,0:T(8,128)(2,1)}), bf16[8,192,768]{2,1,0:T(8,128)(2,1)}, u32[]{:S(2)}, u32[]{:S(2)}) %all-to-all-start.2) | async-done | bytes 2359328 | tf_op jit(solution)/shard_map/all_to_all | solution.py:341
  180.0 22.1 %fusion.6 = bf16[1536,3072]{1,0:T(8,128)(2,1)S(1)} fusion(f32[1536,3072]{1,0:T(8,128)} %fusion.15, bf16[1536,768]{1,0:T(8,128)(2,1)} %bitcast.39, bf16[1,3072,768]{2,1,0:T(8,128)(2,1)} %param.21), kind=kOutput, calls=%fused_computation.9 | convolution fusion | flops 7342129152 | bytes 35389440 | tf_op jit(solution)/shard_map/dot_general | solution.py:51
  202.0 3.6 copy-done.37
  205.7 10.8 %convolution_convert_fusion.1 = bf16[768,3072]{1,0:T(8,128)(2,1)} fusion(bf16[1536,768]{1,0:T(8,128)(2,1)} %bitcast.31, bf16[1536,3072]{1,0:T(8,128)(2,1)S(1)} %fusion.6), kind=kOutput, calls=%fused_computation.13 | convolution fusion | flops 7250116608 | bytes 16515072 | tf_op jit(solution)/shard_map/dot_general | solution.py:59
  219.7 13.8 %fusion.17 = bf16[1536,768]{1,0:T(8,128)(2,1)} fusion(bf16[1536,3072]{1,0:T(8,128)(2,1)} %copy-done.37, bf16[1,768,3072]{2,1,0:T(8,128)(2,1)} %param.20), kind=kOutput, calls=%fused_computation.23 | convolution fusion | flops 7248936960 | bytes 16515072 | tf_op jit(solution)/shard_map/dot_general | solution.py:51
  233.5 4.4 all-to-all-start.3
  237.9 17.1 %fusion.20 = bf16[1536,768]{1,0:T(8,128)(2,1)} fusion(bf16[1,3072,768]{2,1,0:T(8,128)(2,1)} %param.21, f32[1536,3072]{1,0:T(8,128)} %fusion.15), kind=kOutput, calls=%fused_computation.24 | convolution fusion | flops 7291404288 | bytes 25952256 | tf_op jit(solution)/shard_map/dot_general | solution.py:55
  255.0 12.4 %all-to-all-done.3 = bf16[8,192,768]{2,1,0:T(8,128)(2,1)} async-done(((bf16[8,192,768]{2,1,0:T(8,128)(2,1)}), bf16[8,192,768]{2,1,0:T(8,128)(2,1)}, u32[]{:S(2)}, u32[]{:S(2)}) %all-to-all-start.3) | async-done | bytes 2359328 | tf_op jit(solution)/shard_map/all_to_all | solution.py:341
  267.3 4.4 all-to-all-start.1
  271.8 16.4 %convolution_convert_fusion = bf16[3072,768]{1,0:T(8,128)(2,1)} fusion(bf16[1536,768]{1,0:T(8,128)(2,1)} %bitcast.39, f32[1536,3072]{1,0:T(8,128)} %fusion.15), kind=kOutput, calls=%fused_computation.12 | convolution fusion | flops 7292583936 | bytes 25952256 | tf_op jit(solution)/shard_map/dot_general | solution.py:59
  288.2 4.3 multiply_reduce_fusion.1
  297.8 3.4 all-to-all-done.1
  301.2 4.6 add_convert_fusion.1
  310.4 3.1 collective-permute-start.20
  319.3 2.7 collective-permute-start.24
  322.0 2.4 collective-permute-done.17
  324.4 18.7 %collective-permute-done.18 = bf16[256,384]{1,0:T(8,128)(2,1)} collective-permute-done((bf16[256,384]{1,0:T(8,128)(2,1)}, bf16[256,384]{1,0:T(8,128)(2,1)}, u32[]{:S(2)}, u32[]{:S(2)}) %collective-permute-start.18) | collective-permute-done | bytes 196640 | tf_op jit(solution)/shard_map/ppermute | solution.py:231
  344.5 14.9 %attend_back.1 = bf16[1024,1152]{1,0:T(8,128)(2,1)S(1)} custom-call(bf16[1024,1152]{1,0:T(8,128)(2,1)} %copy-done.2, bf16[1024,1152]{1,0:T(8,128)(2,1)} %copy-done.2, bf16[1024,1152]{1,0:T(8,128)(2,1)} %copy-done.2, bf16[1024,384]{1,0:T(8,128)(2,1)S(1)} %copy-done.4, bf16[1024,384]{1,0:T(8,128)(2,1)S(1)} %pad_maximum_fusion.9.datt_ref, ...), custom_call_target="tpu_custom_call" | custom-call | flops 2013265920 | bytes 7077888 | tf_op jit(solution)/shard_map/attend_back/pallas_call | solution.py:191
  361.8 25.4 %collective-permute-start.21 = (bf16[512,768]{1,0:T(8,128)(2,1)S(1)}, bf16[512,768]{1,0:T(8,128)(2,1)S(1)}, u32[]{:S(2)}, u32[]{:S(2)}) collective-permute-start(bf16[512,768]{1,0:T(8,128)(2,1)S(1)} %fusion.47), channel_id=1, source_target_pairs={{0,4},{1,5},{2,6},{3,7},{4,0},{5,1},{6,2},{7,3},{8,12},{9,13},{10,... | collective-permute-start | bytes 2359304 | tf_op jit(solution)/shard_map/ppermute | solution.py:231
  387.1 4.4 fusion.73
  393.0 4.7 %collective-permute-start.23 = (bf16[256,768]{1,0:T(8,128)(2,1)}, bf16[256,768]{1,0:T(8,128)(2,1)}, u32[]{:S(2)}, u32[]{:S(2)}) collective-permute-start(bf16[256,768]{1,0:T(8,128)(2,1)} %get-tuple-element.127), channel_id=1, source_target_pairs={{0,0},{1,1},{2,4},{3,5},{4,2},{5,3},{6,6},{7,7},{8,8},{9,9},{10,12... | collective-permute-start | bytes 1179656 | tf_op jit(solution)/shard_map/ppermute | solution.py:231
  398.0 2.3 pad_maximum_fusion
  401.0 6.0 %collective-permute-done.22 = bf16[256,768]{1,0:T(8,128)(2,1)S(1)} collective-permute-done((bf16[256,768]{1,0:T(8,128)(2,1)}, bf16[256,768]{1,0:T(8,128)(2,1)S(1)}, u32[]{:S(2)}, u32[]{:S(2)}) %collective-permute-start.22) | collective-permute-done | bytes 393248 | tf_op jit(solution)/shard_map/ppermute | solution.py:231
  408.2 6.4 %collective-permute-done.25 = bf16[2,96,1664]{2,1,0:T(8,128)(2,1)S(1)} collective-permute-done((bf16[2,96,1664]{2,1,0:T(8,128)(2,1)S(1)}, bf16[2,96,1664]{2,1,0:T(8,128)(2,1)S(1)}, u32[]{:S(2)}, u32[]{:S(2)}) %collective-permute-start.25) | collective-permute-done | bytes 639008 | tf_op jit(solution)/shard_map/ppermute | solution.py:231
  417.3 4.6 collective-permute-done.26
  422.3 7.9 %collective-permute-start.29 = (bf16[96,1664]{1,0:T(8,128)(2,1)S(1)}, bf16[96,1664]{1,0:T(8,128)(2,1)S(1)}, u32[]{:S(2)}, u32[]{:S(2)}) collective-permute-start(bf16[96,1664]{1,0:T(8,128)(2,1)S(1)} %get-tuple-element.106), channel_id=1, source_target_pairs={{0,4},{1,5},{2,6},{3,7},{4,0},{5,1},{6,2},{7,3},{8,12},{9,13},{10,... | collective-permute-start | bytes 958472 | tf_op jit(solution)/shard_map/ppermute | solution.py:231
  438.0 2.6 collective-permute-done.32
  440.6 6.9 %collective-permute-done.31 = bf16[24,3200]{1,0:T(8,128)(2,1)S(1)} collective-permute-done((bf16[24,3200]{1,0:T(8,128)(2,1)S(1)}, bf16[24,3200]{1,0:T(8,128)(2,1)S(1)}, u32[]{:S(2)}, u32[]{:S(2)}) %collective-permute-start.31) | collective-permute-done | bytes 153632 | tf_op jit(solution)/shard_map/ppermute | solution.py:231
  449.7 2.9 bitcast_convert_fusion.1
  452.6 2.8 bitcast_convert_fusion
  (249 shorter events, 65.2 us)
Async XLA Ops:
  10.0 9.7 %collective-permute-start.3 = (bf16[24,1664]{1,0:T(8,128)(2,1)S(1)}, bf16[24,1664]{1,0:T(8,128)(2,1)S(1)}, u32[]{:S(2)}, u32[]{:S(2)}) collective-permute-start(bf16[24,1664]{1,0:T(8,128)(2,1)S(1)} %broadcast_select_fusion.29), channel_id=1, source_target_pairs={{0,4},{1,5},{2,6},{3,7},{4,0},{5,1},{6,2},{7,3},{8,12},{9,13},{10,... | collective-permute-start | bytes 239624 | tf_op jit(solution)/shard_map/ppermute | solution.py:231
  11.7 35.4 %collective-permute-start = (bf16[256,768]{1,0:T(8,128)(2,1)S(1)}, bf16[256,768]{1,0:T(8,128)(2,1)S(1)}, u32[]{:S(2)}, u32[]{:S(2)}) collective-permute-start(bf16[256,768]{1,0:T(8,128)(2,1)S(1)} %get-tuple-element.148), channel_id=1, source_target_pairs={{0,1},{1,0},{2,5},{3,4},{4,3},{5,2},{6,7},{7,6},{8,9},{9,8},{10,13... | collective-permute-start | bytes 1179656 | tf_op jit(solution)/shard_map/ppermute | solution.py:231
  14.3 10.1 %collective-permute-start.11 = (s32[2,1024]{1,0:T(2,128)S(1)}, s32[2,1024]{1,0:T(2,128)S(1)}, u32[]{:S(2)}, u32[]{:S(2)}) collective-permute-start(s32[2,1024]{1,0:T(2,128)S(1)} %copy-done.35), channel_id=1, source_target_pairs={{0,4},{1,5},{2,6},{3,7},{4,0},{5,1},{6,2},{7,3},{8,12},{9,13},{10,... | collective-permute-start | bytes 24584 | tf_op jit(solution)/shard_map/ppermute | solution.py:231
  19.7 10.1 %collective-permute-start.4 = (bf16[2,24,1664]{2,1,0:T(8,128)(2,1)S(1)}, bf16[2,24,1664]{2,1,0:T(8,128)(2,1)S(1)}, u32[]{:S(2)}, u32[]{:S(2)}) collective-permute-start(bf16[2,24,1664]{2,1,0:T(8,128)(2,1)S(1)} %pad_maximum_fusion.15), channel_id=1, source_target_pairs={{0,3},{1,2},{2,1},{3,0},{4,7},{5,6},{6,5},{7,4},{8,11},{9,10},{10,... | collective-permute-start | bytes 479240 | tf_op jit(solution)/shard_map/ppermute | solution.py:231
  20.3 23.4 %collective-permute-start.5 = (bf16[2,24,1664]{2,1,0:T(8,128)(2,1)S(1)}, bf16[2,24,1664]{2,1,0:T(8,128)(2,1)S(1)}, u32[]{:S(2)}, u32[]{:S(2)}) collective-permute-start(bf16[2,24,1664]{2,1,0:T(8,128)(2,1)S(1)} %pad_maximum_fusion.15), channel_id=1, source_target_pairs={{0,2},{1,3},{2,0},{3,1},{4,6},{5,7},{6,4},{7,5},{8,10},{9,11},{10,... | collective-permute-start | bytes 479240 | tf_op jit(solution)/shard_map/ppermute | solution.py:231
  20.8 22.9 %collective-permute-start.6 = (bf16[2,24,1664]{2,1,0:T(8,128)(2,1)S(1)}, bf16[2,24,1664]{2,1,0:T(8,128)(2,1)S(1)}, u32[]{:S(2)}, u32[]{:S(2)}) collective-permute-start(bf16[2,24,1664]{2,1,0:T(8,128)(2,1)S(1)} %pad_maximum_fusion.15), channel_id=1, source_target_pairs={{0,1},{1,0},{2,3},{3,2},{4,5},{5,4},{6,7},{7,6},{8,9},{9,8},{10,11... | collective-permute-start | bytes 479240 | tf_op jit(solution)/shard_map/ppermute | solution.py:231
  24.5 22.6 %collective-permute-start.1 = (bf16[256,768]{1,0:T(8,128)(2,1)S(1)}, bf16[256,768]{1,0:T(8,128)(2,1)S(1)}, u32[]{:S(2)}, u32[]{:S(2)}) collective-permute-start(bf16[256,768]{1,0:T(8,128)(2,1)S(1)} %get-tuple-element.149), channel_id=1, source_target_pairs={{0,0},{1,1},{2,4},{3,5},{4,2},{5,3},{6,6},{7,7},{8,8},{9,9},{10,12... | collective-permute-start | bytes 1179656 | tf_op jit(solution)/shard_map/ppermute | solution.py:231
  44.0 7.4 %collective-permute-start.7 = (bf16[4,24,1664]{2,1,0:T(8,128)(2,1)S(1)}, bf16[4,24,1664]{2,1,0:T(8,128)(2,1)S(1)}, u32[]{:S(2)}, u32[]{:S(2)}) collective-permute-start(bf16[4,24,1664]{2,1,0:T(8,128)(2,1)S(1)} %get-tuple-element.152), channel_id=1, source_target_pairs={{0,8},{1,9},{2,10},{3,11},{4,12},{5,13},{6,14},{7,15},{8,0},{9,1},... | collective-permute-start | bytes 958472 | tf_op jit(solution)/shard_map/ppermute | solution.py:231
  45.6 7.2 %collective-permute-start.9 = (bf16[4,24,1664]{2,1,0:T(8,128)(2,1)S(1)}, bf16[4,24,1664]{2,1,0:T(8,128)(2,1)S(1)}, u32[]{:S(2)}, u32[]{:S(2)}) collective-permute-start(bf16[4,24,1664]{2,1,0:T(8,128)(2,1)S(1)} %get-tuple-element.153), channel_id=1, source_target_pairs={{0,16},{1,17},{2,18},{3,19},{4,20},{5,21},{6,22},{7,23},{8,24},{9,... | collective-permute-start | bytes 958472 | tf_op jit(solution)/shard_map/ppermute | solution.py:231
  47.2 8.0 %collective-permute-start.2 = (bf16[512,768]{1,0:T(8,128)(2,1)S(1)}, bf16[512,768]{1,0:T(8,128)(2,1)S(1)}, u32[]{:S(2)}, u32[]{:S(2)}) collective-permute-start(bf16[512,768]{1,0:T(8,128)(2,1)S(1)} %pad_maximum_fusion.7), channel_id=1, source_target_pairs={{0,4},{1,5},{2,6},{3,7},{4,0},{5,1},{6,2},{7,3},{8,12},{9,13},{10,... | collective-permute-start | bytes 2359304 | tf_op jit(solution)/shard_map/ppermute | solution.py:231
  53.0 13.2 %collective-permute-start.10 = (bf16[2,4,24,1664]{3,2,1,0:T(8,128)(2,1)S(1)}, bf16[2,4,24,1664]{3,2,1,0:T(8,128)(2,1)S(1)}, u32[]{:S(2)}, u32[]{:S(2)}) collective-permute-start(bf16[2,4,24,1664]{3,2,1,0:T(8,128)(2,1)S(1)} %pad_maximum_fusion.14), channel_id=1, source_target_pairs={{0,8},{1,9},{2,10},{3,11},{4,12},{5,13},{6,14},{7,15},{8,0},{9,1},... | collective-permute-start | bytes 1916936 | tf_op jit(solution)/shard_map/ppermute | solution.py:231
  53.5 13.0 %collective-permute-start.8 = (bf16[2,4,24,1664]{3,2,1,0:T(8,128)(2,1)S(1)}, bf16[2,4,24,1664]{3,2,1,0:T(8,128)(2,1)S(1)}, u32[]{:S(2)}, u32[]{:S(2)}) collective-permute-start(bf16[2,4,24,1664]{3,2,1,0:T(8,128)(2,1)S(1)} %pad_maximum_fusion.13), channel_id=1, source_target_pairs={{0,16},{1,17},{2,18},{3,19},{4,20},{5,21},{6,22},{7,23},{8,24},{9,... | collective-permute-start | bytes 1916936 | tf_op jit(solution)/shard_map/ppermute | solution.py:231
  67.3 35.7 %copy-start.17 = (bf16[4,2,96,1664]{3,2,1,0:T(8,128)(2,1)}, bf16[4,2,96,1664]{3,2,1,0:T(8,128)(2,1)S(1)}, u32[]{:S(2)}) copy-start(bf16[4,2,96,1664]{3,2,1,0:T(8,128)(2,1)S(1)} %copy.173) | copy-start | bytes 7667716
  67.4 35.6 %collective-permute-start.16 = (bf16[768,384]{1,0:T(8,128)(2,1)S(1)}, bf16[768,384]{1,0:T(8,128)(2,1)S(1)}, u32[]{:S(2)}, u32[]{:S(2)}) collective-permute-start(bf16[768,384]{1,0:T(8,128)(2,1)S(1)} %slice.153), channel_id=1, source_target_pairs={{0,4},{1,5},{2,6},{3,7},{4,0},{5,1},{6,2},{7,3},{8,12},{9,13},{10,... | collective-permute-start | bytes 1769480 | tf_op jit(solution)/shard_map/ppermute | solution.py:231
  85.2 18.0 %copy-start.3 = (bf16[1024,384]{1,0:T(8,128)(2,1)}, bf16[1024,384]{1,0:T(8,128)(2,1)S(1)}, u32[]{:S(2)}) copy-start(bf16[1024,384]{1,0:T(8,128)(2,1)S(1)} %get-tuple-element.10.att_ref) | copy-start | bytes 2359300
  85.3 17.9 %copy-start.5 = (bf16[2,256,768]{2,1,0:T(8,128)(2,1)S(1)}, bf16[2,256,768]{2,1,0:T(8,128)(2,1)}, u32[]{:S(2)}) copy-start(bf16[2,256,768]{2,1,0:T(8,128)(2,1)} %param.11) | copy-start | bytes 2359300
  85.3 11.2 %collective-permute-start.12 = (bf16[256,384]{1,0:T(8,128)(2,1)S(1)}, bf16[256,384]{1,0:T(8,128)(2,1)S(1)}, u32[]{:S(2)}, u32[]{:S(2)}) collective-permute-start(bf16[256,384]{1,0:T(8,128)(2,1)S(1)} %get-tuple-element.145), channel_id=1, source_target_pairs={{0,3},{1,2},{2,7},{3,6},{4,1},{5,0},{6,5},{7,4},{8,11},{9,10},{10,... | collective-permute-start | bytes 589832 | tf_op jit(solution)/shard_map/ppermute | solution.py:231
  91.2 9.5 %collective-permute-start.13 = (bf16[256,384]{1,0:T(8,128)(2,1)S(1)}, bf16[256,384]{1,0:T(8,128)(2,1)S(1)}, u32[]{:S(2)}, u32[]{:S(2)}) collective-permute-start(bf16[256,384]{1,0:T(8,128)(2,1)S(1)} %get-tuple-element.144), channel_id=1, source_target_pairs={{0,2},{1,3},{2,6},{3,7},{4,0},{5,1},{6,4},{7,5},{8,10},{9,11},{10,... | collective-permute-start | bytes 589832 | tf_op jit(solution)/shard_map/ppermute | solution.py:231
  91.9 11.0 %collective-permute-start.14 = (bf16[256,384]{1,0:T(8,128)(2,1)S(1)}, bf16[256,384]{1,0:T(8,128)(2,1)S(1)}, u32[]{:S(2)}, u32[]{:S(2)}) collective-permute-start(bf16[256,384]{1,0:T(8,128)(2,1)S(1)} %get-tuple-element.142), channel_id=1, source_target_pairs={{0,1},{1,0},{2,5},{3,4},{4,3},{5,2},{6,7},{7,6},{8,9},{9,8},{10,13... | collective-permute-start | bytes 589832 | tf_op jit(solution)/shard_map/ppermute | solution.py:231
  91.9 11.0 %collective-permute-start.15 = (bf16[256,384]{1,0:T(8,128)(2,1)S(1)}, bf16[256,384]{1,0:T(8,128)(2,1)S(1)}, u32[]{:S(2)}, u32[]{:S(2)}) collective-permute-start(bf16[256,384]{1,0:T(8,128)(2,1)S(1)} %get-tuple-element.143), channel_id=1, source_target_pairs={{0,0},{1,1},{2,4},{3,5},{4,2},{5,3},{6,6},{7,7},{8,8},{9,9},{10,12... | collective-permute-start | bytes 589832 | tf_op jit(solution)/shard_map/ppermute | solution.py:231
  107.7 38.4 %all-to-all-start = ((bf16[8,192,768]{2,1,0:T(8,128)(2,1)}), bf16[8,192,768]{2,1,0:T(8,128)(2,1)}, u32[]{:S(2)}, u32[]{:S(2)}) async-start(bf16[8,192,768]{2,1,0:T(8,128)(2,1)} %bitcast.256), calls=%async_computation | async-start | bytes 4718592 | tf_op jit(solution)/shard_map/all_to_all | solution.py:341
  146.1 33.9 %all-to-all-start.2 = ((bf16[8,192,768]{2,1,0:T(8,128)(2,1)}), bf16[8,192,768]{2,1,0:T(8,128)(2,1)}, u32[]{:S(2)}, u32[]{:S(2)}) async-start(bf16[8,192,768]{2,1,0:T(8,128)(2,1)} %bitcast.255), calls=%async_computation.2 | async-start | bytes 4718592 | tf_op jit(solution)/shard_map/all_to_all | solution.py:341
  150.5 299.2 %reduce-scatter.3.cloned.1.call-start = ((), (), s32[]{:S(2)}) async-start(), calls=%async_computation.6 | async-start | bytes 5898240 | tf_op jit(solution)/shard_map/reduce_scatter | solution.py:383
  233.5 33.8 %all-to-all-start.3 = ((bf16[8,192,768]{2,1,0:T(8,128)(2,1)}), bf16[8,192,768]{2,1,0:T(8,128)(2,1)}, u32[]{:S(2)}, u32[]{:S(2)}) async-start(bf16[8,192,768]{2,1,0:T(8,128)(2,1)} %bitcast.257), calls=%async_computation.3 | async-start | bytes 4718592 | tf_op jit(solution)/shard_map/all_to_all | solution.py:341
  267.3 33.8 %all-to-all-start.1 = ((bf16[8,192,768]{2,1,0:T(8,128)(2,1)}), bf16[8,192,768]{2,1,0:T(8,128)(2,1)}, u32[]{:S(2)}, u32[]{:S(2)}) async-start(bf16[8,192,768]{2,1,0:T(8,128)(2,1)} %bitcast.254), calls=%async_computation.1 | async-start | bytes 4718592 | tf_op jit(solution)/shard_map/all_to_all | solution.py:341
  271.7 180.9 %reduce-scatter.5.cloned.1.call-start = ((), (), s32[]{:S(2)}) async-start(), calls=%async_computation.7 | async-start | bytes 5898240 | tf_op jit(solution)/shard_map/reduce_scatter | solution.py:377
  310.3 14.1 %collective-permute-start.17 = (bf16[256,384]{1,0:T(8,128)(2,1)}, bf16[256,384]{1,0:T(8,128)(2,1)}, u32[]{:S(2)}, u32[]{:S(2)}) collective-permute-start(bf16[256,384]{1,0:T(8,128)(2,1)} %get-tuple-element.135), channel_id=1, source_target_pairs={{0,5},{1,4},{2,1},{3,0},{4,7},{5,6},{6,3},{7,2},{8,13},{9,12},{10,... | collective-permute-start | bytes 589832 | tf_op jit(solution)/shard_map/ppermute | solution.py:231
  310.3 32.7 %collective-permute-start.18 = (bf16[256,384]{1,0:T(8,128)(2,1)}, bf16[256,384]{1,0:T(8,128)(2,1)}, u32[]{:S(2)}, u32[]{:S(2)}) collective-permute-start(bf16[256,384]{1,0:T(8,128)(2,1)} %get-tuple-element.134), channel_id=1, source_target_pairs={{0,4},{1,5},{2,0},{3,1},{4,6},{5,7},{6,2},{7,3},{8,12},{9,13},{10,... | collective-permute-start | bytes 589832 | tf_op jit(solution)/shard_map/ppermute | solution.py:231
  310.3 32.7 %collective-permute-start.19 = (bf16[256,384]{1,0:T(8,128)(2,1)}, bf16[256,384]{1,0:T(8,128)(2,1)}, u32[]{:S(2)}, u32[]{:S(2)}) collective-permute-start(bf16[256,384]{1,0:T(8,128)(2,1)} %get-tuple-element.132), channel_id=1, source_target_pairs={{0,1},{1,0},{2,5},{3,4},{4,3},{5,2},{6,7},{7,6},{8,9},{9,8},{10,13... | collective-permute-start | bytes 589832 | tf_op jit(solution)/shard_map/ppermute | solution.py:231
  310.4 32.7 %collective-permute-start.20 = (bf16[256,384]{1,0:T(8,128)(2,1)}, bf16[256,384]{1,0:T(8,128)(2,1)}, u32[]{:S(2)}, u32[]{:S(2)}) collective-permute-start(bf16[256,384]{1,0:T(8,128)(2,1)} %get-tuple-element.133), channel_id=1, source_target_pairs={{0,0},{1,1},{2,4},{3,5},{4,2},{5,3},{6,6},{7,7},{8,8},{9,9},{10,12... | collective-permute-start | bytes 589832 | tf_op jit(solution)/shard_map/ppermute | solution.py:231
  317.1 27.3 %copy-start.4 = (bf16[1024,384]{1,0:T(8,128)(2,1)S(1)}, bf16[1024,384]{1,0:T(8,128)(2,1)}, u32[]{:S(2)}) copy-start(bf16[1024,384]{1,0:T(8,128)(2,1)} %copy-done.3) | copy-start | bytes 2359300
  319.3 72.2 %collective-permute-start.24 = (bf16[768,384]{1,0:T(8,128)(2,1)}, bf16[768,384]{1,0:T(8,128)(2,1)S(1)}, u32[]{:S(2)}, u32[]{:S(2)}) collective-permute-start(bf16[768,384]{1,0:T(8,128)(2,1)} %bitcast.264), channel_id=1, source_target_pairs={{0,4},{1,5},{2,6},{3,7},{4,0},{5,1},{6,2},{7,3},{8,12},{9,13},{10,... | collective-permute-start | bytes 1769480 | tf_op jit(solution)/shard_map/ppermute | solution.py:231
  344.5 14.9 %copy-start.18 = (bf16[4,2,96,1664]{3,2,1,0:T(8,128)(2,1)S(1)}, bf16[4,2,96,1664]{3,2,1,0:T(8,128)(2,1)}, u32[]{:S(2)}) copy-start(bf16[4,2,96,1664]{3,2,1,0:T(8,128)(2,1)} %copy-done.17) | copy-start | bytes 7667716
  359.4 27.7 %copy-start.12 = (bf16[512,768]{1,0:T(8,128)(2,1)S(1)}, bf16[512,768]{1,0:T(8,128)(2,1)}, u32[]{:S(2)}) copy-start(bf16[512,768]{1,0:T(8,128)(2,1)} %copy-done.10) | copy-start | bytes 2359300
  359.4 27.7 %copy-start.31 = (f32[768]{0:T(1024)S(1)}, f32[768]{0:T(1024)}, u32[]{:S(2)}) copy-start(f32[768]{0:T(1024)} %copy-done.30) | copy-start | bytes 9220
  359.4 27.7 %copy-start.34 = (f32[768]{0:T(1024)S(1)}, f32[768]{0:T(1024)}, u32[]{:S(2)}) copy-start(f32[768]{0:T(1024)} %copy-done.33) | copy-start | bytes 9220
  361.7 29.8 %copy-start.19 = (f32[768,1,384]{2,0,1:T(8,128)S(1)}, f32[768,1,384]{2,0,1:T(8,128)}, u32[]{:S(2)}) copy-start(f32[768,1,384]{2,0,1:T(8,128)} %copy.178) | copy-start | bytes 3538948
  361.8 29.9 %collective-permute-start.21 = (bf16[512,768]{1,0:T(8,128)(2,1)S(1)}, bf16[512,768]{1,0:T(8,128)(2,1)S(1)}, u32[]{:S(2)}, u32[]{:S(2)}) collective-permute-start(bf16[512,768]{1,0:T(8,128)(2,1)S(1)} %fusion.47), channel_id=1, source_target_pairs={{0,4},{1,5},{2,6},{3,7},{4,0},{5,1},{6,2},{7,3},{8,12},{9,13},{10,... | collective-permute-start | bytes 2359304 | tf_op jit(solution)/shard_map/ppermute | solution.py:231
  393.0 14.0 %collective-permute-start.22 = (bf16[256,768]{1,0:T(8,128)(2,1)}, bf16[256,768]{1,0:T(8,128)(2,1)S(1)}, u32[]{:S(2)}, u32[]{:S(2)}) collective-permute-start(bf16[256,768]{1,0:T(8,128)(2,1)} %get-tuple-element.126), channel_id=1, source_target_pairs={{0,1},{1,0},{2,5},{3,4},{4,3},{5,2},{6,7},{7,6},{8,9},{9,8},{10,13... | collective-permute-start | bytes 1179656 | tf_op jit(solution)/shard_map/ppermute | solution.py:231
  393.0 14.0 %collective-permute-start.23 = (bf16[256,768]{1,0:T(8,128)(2,1)}, bf16[256,768]{1,0:T(8,128)(2,1)}, u32[]{:S(2)}, u32[]{:S(2)}) collective-permute-start(bf16[256,768]{1,0:T(8,128)(2,1)} %get-tuple-element.127), channel_id=1, source_target_pairs={{0,0},{1,1},{2,4},{3,5},{4,2},{5,3},{6,6},{7,7},{8,8},{9,9},{10,12... | collective-permute-start | bytes 1179656 | tf_op jit(solution)/shard_map/ppermute | solution.py:231
  400.8 13.9 %collective-permute-start.25 = (bf16[2,96,1664]{2,1,0:T(8,128)(2,1)S(1)}, bf16[2,96,1664]{2,1,0:T(8,128)(2,1)S(1)}, u32[]{:S(2)}, u32[]{:S(2)}) collective-permute-start(bf16[2,96,1664]{2,1,0:T(8,128)(2,1)S(1)} %fusion.52), channel_id=1, source_target_pairs={{0,8},{1,9},{2,10},{3,11},{4,12},{5,13},{6,14},{7,15},{8,0},{9,1},... | collective-permute-start | bytes 1916936 | tf_op jit(solution)/shard_map/ppermute | solution.py:231
  400.9 14.0 %collective-permute-start.27 = (bf16[2,96,1664]{2,1,0:T(8,128)(2,1)S(1)}, bf16[2,96,1664]{2,1,0:T(8,128)(2,1)S(1)}, u32[]{:S(2)}, u32[]{:S(2)}) collective-permute-start(bf16[2,96,1664]{2,1,0:T(8,128)(2,1)S(1)} %fusion.53), channel_id=1, source_target_pairs={{0,16},{1,17},{2,18},{3,19},{4,20},{5,21},{6,22},{7,23},{8,24},{9,... | collective-permute-start | bytes 1916936 | tf_op jit(solution)/shard_map/ppermute | solution.py:231
  414.8 7.1 %collective-permute-start.26 = (bf16[96,1664]{1,0:T(8,128)(2,1)S(1)}, bf16[96,1664]{1,0:T(8,128)(2,1)S(1)}, u32[]{:S(2)}, u32[]{:S(2)}) collective-permute-start(bf16[96,1664]{1,0:T(8,128)(2,1)S(1)} %fusion.60), channel_id=1, source_target_pairs={{0,16},{1,17},{2,18},{3,19},{4,20},{5,21},{6,22},{7,23},{8,24},{9,... | collective-permute-start | bytes 958472 | tf_op jit(solution)/shard_map/ppermute | solution.py:231
  415.1 7.1 %collective-permute-start.28 = (bf16[96,1664]{1,0:T(8,128)(2,1)S(1)}, bf16[96,1664]{1,0:T(8,128)(2,1)S(1)}, u32[]{:S(2)}, u32[]{:S(2)}) collective-permute-start(bf16[96,1664]{1,0:T(8,128)(2,1)S(1)} %fusion.61), channel_id=1, source_target_pairs={{0,8},{1,9},{2,10},{3,11},{4,12},{5,13},{6,14},{7,15},{8,0},{9,1},... | collective-permute-start | bytes 958472 | tf_op jit(solution)/shard_map/ppermute | solution.py:231
  422.3 9.1 %collective-permute-start.29 = (bf16[96,1664]{1,0:T(8,128)(2,1)S(1)}, bf16[96,1664]{1,0:T(8,128)(2,1)S(1)}, u32[]{:S(2)}, u32[]{:S(2)}) collective-permute-start(bf16[96,1664]{1,0:T(8,128)(2,1)S(1)} %get-tuple-element.106), channel_id=1, source_target_pairs={{0,4},{1,5},{2,6},{3,7},{4,0},{5,1},{6,2},{7,3},{8,12},{9,13},{10,... | collective-permute-start | bytes 958472 | tf_op jit(solution)/shard_map/ppermute | solution.py:231
  431.8 8.8 %collective-permute-start.32 = (bf16[24,3200]{1,0:T(8,128)(2,1)S(1)}, bf16[24,3200]{1,0:T(8,128)(2,1)S(1)}, u32[]{:S(2)}, u32[]{:S(2)}) collective-permute-start(bf16[24,3200]{1,0:T(8,128)(2,1)S(1)} %get-tuple-element.118), channel_id=1, source_target_pairs={{0,3},{1,2},{2,1},{3,0},{4,7},{5,6},{6,5},{7,4},{8,11},{9,10},{10,... | collective-permute-start | bytes 460808 | tf_op jit(solution)/shard_map/ppermute | solution.py:231
  434.0 13.5 %collective-permute-start.31 = (bf16[24,3200]{1,0:T(8,128)(2,1)S(1)}, bf16[24,3200]{1,0:T(8,128)(2,1)S(1)}, u32[]{:S(2)}, u32[]{:S(2)}) collective-permute-start(bf16[24,3200]{1,0:T(8,128)(2,1)S(1)} %get-tuple-element.119), channel_id=1, source_target_pairs={{0,2},{1,3},{2,0},{3,1},{4,6},{5,7},{6,4},{7,5},{8,10},{9,11},{10,... | collective-permute-start | bytes 460808 | tf_op jit(solution)/shard_map/ppermute | solution.py:231
  434.0 13.5 %collective-permute-start.30 = (bf16[24,3200]{1,0:T(8,128)(2,1)S(1)}, bf16[24,3200]{1,0:T(8,128)(2,1)S(1)}, u32[]{:S(2)}, u32[]{:S(2)}) collective-permute-start(bf16[24,3200]{1,0:T(8,128)(2,1)S(1)} %get-tuple-element.117), channel_id=1, source_target_pairs={{0,1},{1,0},{2,3},{3,2},{4,5},{5,4},{6,7},{7,6},{8,9},{9,8},{10,11... | collective-permute-start | bytes 460808 | tf_op jit(solution)/shard_map/ppermute | solution.py:231
  (29 other events, 133.1 us)
Sparse Core Ops, SparseCore 0:
  216.6 84.1 reduce-scatter.2
  303.2 101.0 reduce-scatter.4
